TPU v7x, 32 devices: a whole 2x2x4 slice. The times are simulated.
32 devices in a mesh: row: 4 (over x, core), col: 8 (over z, y).
Axes of the slice: x: 2, y: 2, z: 4, core: 2. Of those that a mesh axis runs over, the one named last changes fastest.
Arguments:
- density: bfloat16 [2048, 2048], P('row', 'col'), may hold values from -2 to 2
- core_ham: float32 [2048, 2048], P('row', 'col'), may hold values from -6 to 6
- block_mask: int32 [32, 32], P('row', 'col'), may hold values 0 or 1
- send_blocks: int32 [32, 32, 8], P(('row', 'col')), may hold values from -1 to 31, as said below
- task_atoms: int32 [2, 32, 32, 8], P(None, ('row', 'col')), may hold values from 0 to 15
- basis: bfloat16 [32, 1024, 2048], P(('row', 'col')), may hold values from -0.375 to 0.375
- v_loc: float32 [32, 2048], P(('row', 'col')), may hold values from -6 to 6
Outputs:
- ks_matrix: float32 [2048, 2048], P('row', 'col')
- sign_step: float32 [2048, 2048], P('row', 'col')
Inputs may be any that keep to these rules, and one draw needn't show every extreme that they name: In each list send_blocks[o, e] the live entries come first and the rest are -1; every list has one live entry or more, and in every draw some sub-slab receives all 8 slots live from every owner.
All inputs are finite; a program needn't handle non-finite values. No bound on the sum of `block_mask` on one device may be relied on, other than what follows from the above.
Results may differ from a plain program's by a relative error of at most 0.0048.
Values may be sent and summed in bfloat16 or wider, within the bound.
A program may use at most 64 MiB of HBM per device.

v0:
```python
import math

import jax
import jax.numpy as jnp
from jax import lax
from jax.sharding import PartitionSpec as P

ATOMS = 16


block_edge = 64


def send_density(outgoing):
    return lax.all_to_all(outgoing, ("row", "col"), split_axis=0, concat_axis=0, tiled=True)


def send_back(returning):
    return lax.all_to_all(returning, ("row", "col"), split_axis=0, concat_axis=0, tiled=True)


def panel_product(left_panel, right_tile):
    return jnp.dot(
        left_panel,
        lax.all_gather(right_tile, "row", axis=0, tiled=True),
        preferred_element_type=jnp.float32,
    )


def body(density, core_ham, block_mask, send_blocks, task_atoms, basis, v_loc):
    row_count = lax.axis_size("row")
    col_count = lax.axis_size("col")
    device_count = row_count * col_count
    block_rows = density.shape[0] // block_edge
    block_cols = density.shape[1] // block_edge
    local_count = block_rows * block_cols
    area = block_edge * block_edge
    slot_count = send_blocks.shape[2]
    dens_blocks = (
        density.reshape(block_rows, block_edge, block_cols, block_edge)
        .transpose(0, 2, 1, 3)
        .reshape(local_count, area)
    )
    slots = send_blocks[0]
    live = (slots >= 0).reshape(-1)
    safe = jnp.maximum(slots, 0).reshape(-1)
    picked = jnp.take(dens_blocks, safe, axis=0) * live[:, None].astype(jnp.bfloat16)
    outgoing = picked.reshape(device_count, slot_count, area)
    received = send_density(outgoing)
    atoms = task_atoms[:, 0]
    pair = (atoms[0] * ATOMS + atoms[1]).reshape(-1)
    pair_ids = jnp.arange(ATOMS * ATOMS, dtype=jnp.int32)
    onehot = (pair[:, None] == pair_ids[None, :]).astype(jnp.bfloat16)
    pair_sum = lax.dot_general(
        onehot,
        received.reshape(-1, area),
        (((0,), (0,)), ((), ())),
        preferred_element_type=jnp.float32,
    )
    pair_mat = (
        pair_sum.reshape(ATOMS, ATOMS, block_edge, block_edge)
        .transpose(0, 2, 1, 3)
        .reshape(ATOMS * block_edge, ATOMS * block_edge)
        .astype(jnp.bfloat16)
    )
    basis_vals = basis[0]
    mixed = jnp.dot(pair_mat, basis_vals, preferred_element_type=jnp.float32)
    rho = jnp.sum(basis_vals * mixed, axis=0)
    pot = v_loc[0] + 0.5 * rho / jnp.sqrt(1.0 + rho * rho)
    weighted = (basis_vals * pot[None, :]).astype(jnp.bfloat16)
    k_all = lax.dot_general(
        weighted, basis_vals, (((1,), (1,)), ((), ())), preferred_element_type=jnp.float32
    )
    k_pairs = (
        k_all.reshape(ATOMS, block_edge, ATOMS, block_edge)
        .transpose(0, 2, 1, 3)
        .reshape(ATOMS * ATOMS, area)
    )
    k_slot = (
        jnp.take(k_pairs, pair, axis=0).astype(jnp.bfloat16).reshape(device_count, slot_count, area)
    )
    returned = send_back(k_slot)
    local_ids = jnp.arange(local_count, dtype=jnp.int32)
    select = (slots.reshape(-1)[None, :] == local_ids[:, None]).astype(jnp.bfloat16)
    ham_blocks = jnp.dot(select, returned.reshape(-1, area), preferred_element_type=jnp.float32)
    ham_tile = (
        ham_blocks.reshape(block_rows, block_cols, block_edge, block_edge)
        .transpose(0, 2, 1, 3)
        .reshape(density.shape)
    )
    ks_matrix = core_ham + ham_tile
    mask = jnp.broadcast_to(
        block_mask.astype(jnp.float32)[:, None, :, None],
        (block_rows, block_edge, block_cols, block_edge),
    ).reshape(density.shape)
    scale = 1.0 / math.sqrt(16.0 * block_rows * row_count)
    x0 = (mask * ks_matrix * scale).astype(jnp.bfloat16)
    left_panel = lax.all_gather(x0, "col", axis=1, tiled=True)
    x2 = (mask * panel_product(left_panel, x0)).astype(jnp.bfloat16)
    x3 = mask * panel_product(left_panel, x2)
    sign_step = (1.5 * x0.astype(jnp.float32) - 0.5 * x3) / scale
    return (ks_matrix, sign_step)


def solution(mesh):
    placed = (
        P("row", "col"),
        P("row", "col"),
        P("row", "col"),
        P(("row", "col"), None, None),
        P(None, ("row", "col"), None, None),
        P(("row", "col"), None, None),
        P(("row", "col"), None),
    )
    return jax.shard_map(
        body,
        mesh=mesh,
        in_specs=placed,
        out_specs=(P("row", "col"), P("row", "col")),
        check_vma=False,
    )
```

profile of v0, /device:TPU:1, one launch (start us, length us, event | category | flops | bytes accessed | tf_op | source)
XLA Modules:
  0.0 273.4 jit_solution(6431178491866917554)
XLA Ops:
  8.7 1.2 reshape.223
  10.7 1.8 gather_fusion
  12.6 1.6 fusion.2
  14.2 7.1 %all-to-all-start = ((bf16[32,8,4096]{2,1,0:T(8,128)(2,1)}), bf16[32,8,4096]{2,1,0:T(8,128)(2,1)S(1)}, u32[]{:S(2)}, u32[]{:S(2)}) async-start(bf16[32,8,4096]{2,1,0:T(8,128)(2,1)} %fusion.2), calls=%async_computation | async-start | bytes 4194304 | tf_op jit(solution)/shard_map/all_to_all | solution.py:15
  21.8 49.1 %all-to-all-done = bf16[32,8,4096]{2,1,0:T(8,128)(2,1)S(1)} async-done(((bf16[32,8,4096]{2,1,0:T(8,128)(2,1)}), bf16[32,8,4096]{2,1,0:T(8,128)(2,1)S(1)}, u32[]{:S(2)}, u32[]{:S(2)}) %all-to-all-start) | async-done | bytes 2097184 | tf_op jit(solution)/shard_map/all_to_all | solution.py:15
  70.8 2.5 copy.23
  73.3 4.8 %convert_bitcast_fusion = bf16[16,64,16,64]{3,2,1,0:T(8,128)(2,1)} fusion(bf16[64,64,256,1]{2,1,0,3:T(8,128)(2,1)} %bitcast.83, s32[16,16]{1,0:T(8,128)S(1)} %multiply_add_fusion, s32[256]{0:T(256)S(1)} %add.88), kind=kOutput, calls=%fused_computation.7 | convolution fusion | flops 537985024 | bytes 4196352 | tf_op jit(solution)/shard_map/dot_general | solution.py:54
  78.1 5.5 %convert_element_type.59 = bf16[1024,1024]{1,0:T(8,128)(2,1)S(1)} reshape(bf16[16,64,16,64]{3,2,1,0:T(8,128)(2,1)} %convert_bitcast_fusion) | data formatting | bytes 4194304 | tf_op jit(solution)/shard_map/convert_element_type | solution.py:64
  83.6 8.1 %multiply_reduce_fusion = f32[2048]{0:T(1024)S(1)} fusion(bf16[1024,1024]{1,0:T(8,128)(2,1)S(1)} %convert_element_type.59, bf16[1,1024,2048]{2,1,0:T(8,128)(2,1)} %param.12), kind=kOutput, calls=%fused_computation.3 | convolution fusion | flops 4301256704 | bytes 6299648 | tf_op jit(solution)/shard_map/dot_general | solution.py:67
  91.8 1.4 multiply_convert_fusion
  93.2 10.4 %convolution_bitcast_fusion = bf16[16,16,64,64]{3,2,1,0:T(8,128)(2,1)} fusion(bf16[16,64,2048,1]{2,1,3,0:T(8,128)(2,1)S(1)} %bitcast.85, bf16[16,64,2048,1]{2,1,0,3:T(8,128)(2,1)S(1)} %bitcast.84), kind=kOutput, calls=%fused_computation.8 | convolution fusion | flops 4294967296 | bytes 10485760 | tf_op jit(solution)/shard_map/dot_general | solution.py:71
  103.6 5.7 %reshape.226 = bf16[256,4096]{1,0:T(8,128)(2,1)S(1)} reshape(bf16[16,16,64,64]{3,2,1,0:T(8,128)(2,1)} %convolution_bitcast_fusion) | data formatting | bytes 4194304 | tf_op jit(solution)/shard_map/reshape | solution.py:77
  109.2 3.2 %gather_fusion.1 = bf16[256,4096]{1,0:T(8,128)(2,1)} fusion(bf16[256,4096]{1,0:T(8,128)(2,1)S(1)} %reshape.226, s32[1024]{0:T(1024)S(1)} %pad_clamp_fusion), kind=kCustom, calls=%fused_computation.1 | custom fusion | bytes 4195328 | tf_op jit(solution)/shard_map/jit(_take)/gather | solution.py:80
  112.4 3.5 %fusion = bf16[32,8,4096]{2,1,0:T(8,128)(2,1)} fusion(bf16[256,4096]{1,0:T(8,128)(2,1)} %gather_fusion.1, pred[32,8]{1,0:T(8,128)(4,1)S(1)} %copy.17), kind=kLoop, calls=%fused_computation.5 | loop fusion | flops 1048576 | bytes 4194560 | tf_op jit(solution)/shard_map/convert_element_type | solution.py:80
  115.9 3.3 %all-to-all-start.1 = ((bf16[32,8,4096]{2,1,0:T(8,128)(2,1)}), bf16[32,8,4096]{2,1,0:T(8,128)(2,1)S(1)}, u32[]{:S(2)}, u32[]{:S(2)}) async-start(bf16[32,8,4096]{2,1,0:T(8,128)(2,1)} %fusion), calls=%async_computation.1 | async-start | bytes 4194304 | tf_op jit(solution)/shard_map/all_to_all | solution.py:19
  120.0 1.4 reshape.229
  121.4 47.5 %all-to-all-done.1 = bf16[32,8,4096]{2,1,0:T(8,128)(2,1)S(1)} async-done(((bf16[32,8,4096]{2,1,0:T(8,128)(2,1)}), bf16[32,8,4096]{2,1,0:T(8,128)(2,1)S(1)}, u32[]{:S(2)}, u32[]{:S(2)}) %all-to-all-start.1) | async-done | bytes 2097184 | tf_op jit(solution)/shard_map/all_to_all | solution.py:19
  168.9 2.5 copy.25
  171.3 2.7 convolution_bitcast_fusion.1
  177.2 14.3 %all-gather.6.cloned.1.call-done = bf16[2048,256]{1,0:T(8,128)(2,1)} async-done(((bf16[512,256]{1,0:T(8,128)(2,1)}), bf16[2048,256]{1,0:T(8,128)(2,1)}) %all-gather.6.cloned.1.call-update) | async-done | bytes 1048592 | tf_op jit(solution)/shard_map/all_gather | solution.py:25
  191.5 52.7 %all-gather.4.cloned.1.call-done = bf16[512,2048]{1,0:T(8,128)(2,1)} async-done(((bf16[512,256]{1,0:T(8,128)(2,1)}), bf16[512,2048]{1,0:T(8,128)(2,1)}) %all-gather.4.cloned.1.call-update) | async-done | bytes 2097168 | tf_op jit(solution)/shard_map/all_gather | solution.py:98
  244.2 3.3 %fusion.6 = bf16[512,256]{1,0:T(8,128)(2,1)} fusion(f32[512,256]{1,0:T(8,128)S(1)} %copy-done.2, bf16[512,2048]{1,0:T(8,128)(2,1)} %all-gather.4.cloned.1.call-done, bf16[2048,256]{1,0:T(8,128)(2,1)} %all-gather.6.cloned.1.call-done), kind=kOutput, calls=%fused_computation.17 | convolution fusion | flops 537133056 | bytes 3932160 | tf_op jit(solution)/shard_map/dot_general | solution.py:23
  247.5 16.1 %all-gather.8.cloned.1.call-done = bf16[2048,256]{1,0:T(8,128)(2,1)} async-done(((bf16[512,256]{1,0:T(8,128)(2,1)}), bf16[2048,256]{1,0:T(8,128)(2,1)}) %all-gather.8.cloned.1.call-update) | async-done | bytes 1048592 | tf_op jit(solution)/shard_map/all_gather | solution.py:25
  263.5 3.4 %fusion.5 = f32[512,256]{1,0:T(8,128)} fusion(f32[512,256]{1,0:T(8,128)S(1)} %copy-done.2, bf16[512,2048]{1,0:T(8,128)(2,1)} %all-gather.4.cloned.1.call-done, bf16[2048,256]{1,0:T(8,128)(2,1)} %all-gather.8.cloned.1.call-done, bf16[512,256]{1,0:T(8,128)(2,1)S(1)} %copy-done.1), kind=kOutput, calls=%fused_computation.16 | convolution fusion | flops 537657344 | bytes 4456448 | tf_op jit(solution)/shard_map/dot_general | solution.py:23
  (50 shorter events, 6.6 us)
Async XLA Ops:
  14.2 7.1 %copy-start.6 = (s32[2,1,32,8]{2,3,1,0:T(8,128)S(1)}, s32[2,1,32,8]{2,3,1,0:T(8,128)}, u32[]{:S(2)}) copy-start(s32[2,1,32,8]{2,3,1,0:T(8,128)} %param.11) | copy-start | bytes 6148
  14.2 56.6 %all-to-all-start = ((bf16[32,8,4096]{2,1,0:T(8,128)(2,1)}), bf16[32,8,4096]{2,1,0:T(8,128)(2,1)S(1)}, u32[]{:S(2)}, u32[]{:S(2)}) async-start(bf16[32,8,4096]{2,1,0:T(8,128)(2,1)} %fusion.2), calls=%async_computation | async-start | bytes 4194304 | tf_op jit(solution)/shard_map/all_to_all | solution.py:15
  83.6 8.2 %copy-start.5 = (f32[1,2048]{1,0:T(1,128)S(1)}, f32[1,2048]{1,0:T(1,128)}, u32[]{:S(2)}) copy-start(f32[1,2048]{1,0:T(1,128)} %param.13) | copy-start | bytes 24580
  83.6 8.2 %copy-start = (bf16[1,1024,2048]{2,1,0:T(8,128)(2,1)S(1)}, bf16[1,1024,2048]{2,1,0:T(8,128)(2,1)}, u32[]{:S(2)}) copy-start(bf16[1,1024,2048]{2,1,0:T(8,128)(2,1)} %param.12) | copy-start | bytes 12582916
  115.9 3.6 %copy-start.4 = (s32[1,32,8]{1,2,0:T(8,128)S(1)}, s32[1,32,8]{1,2,0:T(8,128)}, u32[]{:S(2)}) copy-start(s32[1,32,8]{1,2,0:T(8,128)} %param.10) | copy-start | bytes 3076
  115.9 3.8 %copy-start.7 = (s32[8,4]{0,1:T(4,128)S(1)}, s32[8,4]{0,1:T(4,128)}, u32[]{:S(2)}) copy-start(s32[8,4]{0,1:T(4,128)} %param.9) | copy-start | bytes 388
  115.9 53.0 %all-to-all-start.1 = ((bf16[32,8,4096]{2,1,0:T(8,128)(2,1)}), bf16[32,8,4096]{2,1,0:T(8,128)(2,1)S(1)}, u32[]{:S(2)}, u32[]{:S(2)}) async-start(bf16[32,8,4096]{2,1,0:T(8,128)(2,1)} %fusion), calls=%async_computation.1 | async-start | bytes 4194304 | tf_op jit(solution)/shard_map/all_to_all | solution.py:19
  119.2 72.3 %all-gather.6.cloned.1.call-start = ((), (), s32[]{:S(2)}) async-start(), calls=%async_computation.3 | async-start | bytes 1310720 | tf_op jit(solution)/shard_map/all_gather | solution.py:25
  174.0 1.3 copy-start.2
  174.0 1.3 copy-start.3
  176.3 67.9 %all-gather.4.cloned.1.call-start = ((), (), s32[]{:S(2)}) async-start(), calls=%async_computation.2 | async-start | bytes 2359296 | tf_op jit(solution)/shard_map/all_gather | solution.py:98
  177.1 86.4 %copy-start.1 = (bf16[512,256]{1,0:T(8,128)(2,1)S(1)}, bf16[512,256]{1,0:T(8,128)(2,1)}, u32[]{:S(2)}) copy-start(bf16[512,256]{1,0:T(8,128)(2,1)} %get-tuple-element.2) | copy-start | bytes 786436
  177.1 86.4 %all-gather.8.cloned.1.call-start = ((), (), s32[]{:S(2)}) async-start(), calls=%async_computation.4 | async-start | bytes 1310720 | tf_op jit(solution)/shard_map/all_gather | solution.py:25
Sparse Core Ops, SparseCore 0:
  176.5 14.9 all-gather.5
  194.1 50.0 all-gather.3
  247.6 15.8 all-gather.7
where the time goes:
time: 274 us; the launch traced here: 273 us
  waiting for transfers between devices  180 us (66%)
  matrix products  32.6 us (12%)
  local copies, waits for them, and re-layouts  26.8 us (10%)
  between operations  14 us (5%)
  starting transfers between devices  10.8 us (4%)
  other arithmetic  8.89 us (3%)
    all_gather x1, waiting for transfers between devices, body(): left_panel = lax.all_gather(x0, 'col', axis=1, tiled=True)  52.7 us
    all_to_all x1, waiting for transfers between devices, send_density(): lax.all_to_all(outgoing, ('row', 'col'), split_axis=0, concat_axis=0, til...  49.1 us
    all_to_all x1, waiting for transfers between devices, send_back(): lax.all_to_all(returning, ('row', 'col'), split_axis=0, concat_axis=0, ti...  47.5 us
    all_gather x2, waiting for transfers between devices, panel_product(): lax.all_gather(right_tile, 'row', axis=0, tiled=True)  30.4 us
    dot_general x1, matrix products, body(): lax.dot_general(weighted, basis_vals, (((1,), (1,)), ((), ())), preferred...  10.4 us
    dot_general x1, matrix products, body(): mixed = jnp.dot(pair_mat, basis_vals, preferred_element_type=jnp.float32)  8.14 us
    all_to_all x1, starting transfers between devices, send_density(): lax.all_to_all(outgoing, ('row', 'col'), split_axis=0, concat_axis=0, til...  7.1 us
    dot_general x2, matrix products, panel_product(): jnp.dot(left_panel, lax.all_gather(right_tile, 'row', axis=0, tiled=True)...  6.62 us
  transfers between devices with their start and end apart: 5, of which 5 were waited for; matrix products, arithmetic and copies ran while one was open for 1% of the time, Pallas kernels for 0%

commit v1 on v0

v1 whole, which is shorter than its diff:
```python
import functools
import math

import jax
import jax.numpy as jnp
from jax import lax
from jax.experimental import pallas as pl
from jax.experimental.pallas import tpu as pltpu
from jax.sharding import PartitionSpec as P

ATOMS = 16
EDGE = 64
HALF = EDGE // 2
LANES = 2 * EDGE
CORES = 2
MESH = pl.DeviceIdType.MESH
VMEM_LIMIT = 56 * 1024 * 1024


def low_lanes():
    return lax.broadcasted_iota(jnp.int32, (HALF, LANES), 1) < EDGE


def join_pair(first, second):
    low = low_lanes()
    top = jnp.where(low, first, pltpu.roll(second, EDGE, 1))
    bottom = jnp.where(low, pltpu.roll(first, EDGE, 1), second)
    return top, bottom


def split_pair(top, bottom):
    return join_pair(top, bottom)


def pick_kernel(index_ref, density_ref, out_ref, packed):
    rows, cols = density_ref.shape
    across = cols // EDGE
    count = (rows // EDGE) * across
    packed[count] = jnp.zeros((HALF, LANES), packed.dtype)
    for i in range(rows // EDGE):
        for j in range(0, across, 2):
            lanes = slice(j * EDGE, (j + 2) * EDGE)
            top = density_ref[i * EDGE : i * EDGE + HALF, lanes].astype(jnp.float32)
            bottom = density_ref[i * EDGE + HALF : (i + 1) * EDGE, lanes].astype(jnp.float32)
            first, second = split_pair(top, bottom)
            packed[i * across + j] = first.astype(packed.dtype)
            packed[i * across + j + 1] = second.astype(packed.dtype)

    def copy_slot(slot, carry):
        out_ref[slot] = packed[index_ref[slot]]
        return carry

    lax.fori_loop(0, out_ref.shape[0], copy_slot, 0, unroll=8)


def pick_blocks(index, density):
    count = (density.shape[0] // EDGE) * (density.shape[1] // EDGE)
    return pl.pallas_call(
        pick_kernel,
        out_shape=jax.ShapeDtypeStruct((index.shape[0], HALF, LANES), jnp.bfloat16),
        in_specs=[pl.BlockSpec(memory_space=pltpu.SMEM), pl.BlockSpec(memory_space=pltpu.VMEM)],
        out_specs=pl.BlockSpec(memory_space=pltpu.VMEM),
        scratch_shapes=[pltpu.VMEM((count + 1, HALF, LANES), jnp.bfloat16)],
        compiler_params=pltpu.CompilerParams(vmem_limit_bytes=VMEM_LIMIT),
        name="pick",
    )(index, density)


def grid_kernel(chunk, pair_ref, recv_ref, basis_ref, vloc_ref, out_ref, sums, pair_mat, k_all):
    cells = basis_ref.shape[1]
    sums[...] = jnp.zeros_like(sums)
    k_all[...] = jnp.zeros_like(k_all)

    def add_slot(slot, carry):
        at = pair_ref[slot]
        sums[at] = sums[at] + recv_ref[slot].astype(jnp.float32)
        return carry

    lax.fori_loop(0, recv_ref.shape[0], add_slot, 0, unroll=8)

    def assemble(a, carry):
        row = pl.multiple_of(a * EDGE, EDGE)
        for b in range(0, ATOMS, 2):
            top, bottom = join_pair(sums[a * ATOMS + b], sums[a * ATOMS + b + 1])
            lanes = slice(b * EDGE, (b + 2) * EDGE)
            pair_mat[pl.ds(row, HALF), lanes] = top.astype(jnp.bfloat16)
            pair_mat[pl.ds(row + HALF, HALF), lanes] = bottom.astype(jnp.bfloat16)
        return carry

    lax.fori_loop(0, ATOMS, assemble, 0)

    def integrate(step, carry):
        at = pl.ds(pl.multiple_of(step * chunk, chunk), chunk)
        vals = basis_ref[:, at]
        mixed = jnp.dot(pair_mat[...], vals, preferred_element_type=jnp.float32)
        wide = vals.astype(jnp.float32)
        rho = jnp.sum(wide * mixed, axis=0, keepdims=True)
        pot = vloc_ref[:, at] + 0.5 * rho / jnp.sqrt(1.0 + rho * rho)
        weighted = (wide * pot).astype(jnp.bfloat16)
        k_all[...] += lax.dot_general(
            weighted, vals, (((1,), (1,)), ((), ())), preferred_element_type=jnp.float32
        )
        return carry

    lax.fori_loop(0, cells // chunk, integrate, 0)

    def split(a, carry):
        row = pl.multiple_of(a * EDGE, EDGE)
        for b in range(0, ATOMS, 2):
            lanes = slice(b * EDGE, (b + 2) * EDGE)
            first, second = split_pair(k_all[pl.ds(row, HALF), lanes], k_all[pl.ds(row + HALF, HALF), lanes])
            sums[a * ATOMS + b] = first
            sums[a * ATOMS + b + 1] = second
        return carry

    lax.fori_loop(0, ATOMS, split, 0)

    def give_slot(slot, carry):
        out_ref[slot] = sums[pair_ref[slot]].astype(jnp.bfloat16)
        return carry

    lax.fori_loop(0, out_ref.shape[0], give_slot, 0, unroll=8)


def grid_step(pair, received, basis, v_loc):
    order = ATOMS * EDGE
    chunk = math.gcd(basis.shape[1], 512)
    return pl.pallas_call(
        functools.partial(grid_kernel, chunk),
        out_shape=jax.ShapeDtypeStruct(received.shape, jnp.bfloat16),
        in_specs=[pl.BlockSpec(memory_space=pltpu.SMEM)] + [pl.BlockSpec(memory_space=pltpu.VMEM)] * 3,
        out_specs=pl.BlockSpec(memory_space=pltpu.VMEM),
        scratch_shapes=[
            pltpu.VMEM((ATOMS * ATOMS, HALF, LANES), jnp.float32),
            pltpu.VMEM((order, order), jnp.bfloat16),
            pltpu.VMEM((order, order), jnp.float32),
        ],
        compiler_params=pltpu.CompilerParams(vmem_limit_bytes=VMEM_LIMIT),
        name="grid",
    )(pair, received, basis, v_loc)


def block_masks(mask_ref, i, j):
    low = lax.broadcasted_iota(jnp.int32, (EDGE, LANES), 1) < EDGE
    return jnp.where(low, mask_ref[i, j].astype(jnp.float32), mask_ref[i, j + 1].astype(jnp.float32))


def add_kernel(scale, index_ref, mask_ref, back_ref, core_ref, ks_ref, x0_ref, sums):
    rows, cols = core_ref.shape
    across = cols // EDGE
    sums[...] = jnp.zeros_like(sums)

    def add_slot(slot, carry):
        at = index_ref[slot]
        sums[at] = sums[at] + back_ref[slot].astype(jnp.float32)
        return carry

    lax.fori_loop(0, back_ref.shape[0], add_slot, 0, unroll=8)
    for i in range(rows // EDGE):
        for j in range(0, across, 2):
            lanes = slice(j * EDGE, (j + 2) * EDGE)
            high, mid, low = i * EDGE, i * EDGE + HALF, (i + 1) * EDGE
            top, bottom = join_pair(sums[i * across + j], sums[i * across + j + 1])
            ks_ref[high:mid, lanes] = core_ref[high:mid, lanes] + top
            ks_ref[mid:low, lanes] = core_ref[mid:low, lanes] + bottom
            kept = block_masks(mask_ref, i, j) * ks_ref[high:low, lanes] * scale
            x0_ref[high:low, lanes] = kept.astype(jnp.bfloat16)


def add_back(scale, index, block_mask, returned, core_ham):
    count = (core_ham.shape[0] // EDGE) * (core_ham.shape[1] // EDGE)
    return pl.pallas_call(
        functools.partial(add_kernel, scale),
        out_shape=(
            jax.ShapeDtypeStruct(core_ham.shape, jnp.float32),
            jax.ShapeDtypeStruct(core_ham.shape, jnp.bfloat16),
        ),
        in_specs=[pl.BlockSpec(memory_space=pltpu.SMEM)] * 2 + [pl.BlockSpec(memory_space=pltpu.VMEM)] * 2,
        out_specs=(pl.BlockSpec(memory_space=pltpu.VMEM),) * 2,
        scratch_shapes=[pltpu.VMEM((count + 1, HALF, LANES), jnp.float32)],
        compiler_params=pltpu.CompilerParams(vmem_limit_bytes=VMEM_LIMIT),
        name="add_back",
    )(index, block_mask, returned, core_ham)


class LineGather:
    def __init__(self, held, outer, inner, place, device_at, sems):
        self.held, self.outer, self.inner = held, outer, inner
        self.a, self.b = place // inner, place % inner
        self.device_at = device_at
        self.out_sem, self.in_sem, self.recv_sem = sems
        self.sent = []

    def neighbours(self):
        a, b = self.a, self.b
        return (
            (a > 0, a - 1, b),
            (a < self.outer - 1, a + 1, b),
            (b > 0, a, b - 1),
            (b < self.inner - 1, a, b + 1),
        )

    def send(self, cond, source, target, sem):
        def describe():
            return pltpu.make_async_remote_copy(
                src_ref=self.held.at[source],
                dst_ref=self.held.at[source],
                send_sem=sem,
                recv_sem=self.recv_sem.at[source],
                device_id=self.device_at(target),
                device_id_type=MESH,
            )

        @pl.when(cond)
        def _():
            describe().start()

        self.sent.append((cond, describe))

    def arrive(self, source):
        pltpu.make_async_copy(self.held.at[source], self.held.at[source], self.recv_sem.at[source]).wait()

    def along_inner(self, cond, outer_at, inner_from, step, sem):
        target = self.b + step
        fits = jnp.logical_and(target >= 0, target < self.inner)
        self.send(
            jnp.logical_and(cond, fits), outer_at * self.inner + inner_from, self.a * self.inner + target, sem
        )

    def steps(self):
        a, b, inner = self.a, self.b, self.inner
        for d in range(self.outer):
            for way, step in enumerate((1, -1)):
                if d == 0 and way == 1:
                    have = a >= 0
                    source = a
                else:
                    source = a - d * step
                    have = jnp.logical_and(source >= 0, source < self.outer)
                tile = source * inner + b
                if d > 0:

                    @pl.when(have)
                    def _():
                        self.arrive(tile)

                target = a + step
                fits = jnp.logical_and(target >= 0, target < self.outer)
                self.send(jnp.logical_and(have, fits), tile, target * inner + b, self.out_sem.at[d, way])
                if d > 0 or way == 0:
                    for side, hop in enumerate((1, -1)):
                        self.along_inner(have, source, b, hop, self.in_sem.at[d * 2 + way, side])
            yield
        used = 2 * self.outer
        for e in range(1, inner):
            for outer_at in range(self.outer):
                for way, step in enumerate((1, -1)):
                    origin = b - e * step
                    have = jnp.logical_and(origin >= 0, origin < inner)
                    tile = outer_at * inner + origin

                    @pl.when(have)
                    def _():
                        self.arrive(tile)

                    if e < inner - 1:
                        self.along_inner(have, outer_at, origin, step, self.in_sem.at[used, way])
                if e < inner - 1:
                    used += 1
            yield

    def drain(self):
        for cond, describe in self.sent:

            @pl.when(cond)
            def _():
                describe().wait_send()

    @staticmethod
    def semaphores(outer, inner):
        return [
            pltpu.SemaphoreType.DMA((outer, 2)),
            pltpu.SemaphoreType.DMA((2 * outer + max(inner - 2, 0) * outer, 2)),
            pltpu.SemaphoreType.DMA((outer * inner,)),
        ]


def greet(gathers):
    barrier = pltpu.get_barrier_semaphore()
    count = 0
    for gather in gathers:
        for cond, a, b in gather.neighbours():

            @pl.when(cond)
            def _():
                pl.semaphore_signal(
                    barrier, inc=1, device_id=gather.device_at(a * gather.inner + b), device_id_type=MESH
                )

            count = count + cond.astype(jnp.int32)
    pl.semaphore_wait(barrier, count)


def run_together(*gathers):
    going = [gather.steps() for gather in gathers]
    while going:
        going = [steps for steps in going if next(steps, "end") is None]


def panel_product(left, right, acc):
    height, width = right.shape[1], left.shape[2]
    acc[...] = jnp.zeros_like(acc)
    for j in range(left.shape[0]):
        start = j * width
        part = right[start // height, start % height : start % height + width, :]
        acc[...] += jnp.dot(left[j], part, preferred_element_type=jnp.float32)


def sign_kernel(scale, row_lines, col_lines, mask_ref, x0_ref, out_ref, left, right, second, mask, acc, *sems):
    row, col = lax.axis_index("row"), lax.axis_index("col")
    rows, cols = x0_ref.shape
    along_col = LineGather(left, *col_lines, col, lambda at: (row, at), sems[0:3])
    along_row = LineGather(right, *row_lines, row, lambda at: (at, col), sems[3:6])
    again = LineGather(second, *row_lines, row, lambda at: (at, col), sems[6:9])
    greet([along_col, along_row])
    left[col] = x0_ref[...]
    right[row] = x0_ref[...]
    run_together(along_col, along_row)
    for i in range(rows // EDGE):
        for j in range(0, cols // EDGE, 2):
            mask[i * EDGE : (i + 1) * EDGE, j * EDGE : (j + 2) * EDGE] = block_masks(mask_ref, i, j)
    panel_product(left, right, acc)
    second[row] = (mask[...] * acc[...]).astype(jnp.bfloat16)
    run_together(again)
    panel_product(left, second, acc)
    out_ref[...] = (1.5 * x0_ref[...].astype(jnp.float32) - 0.5 * (mask[...] * acc[...])) / scale
    for gather in (along_col, along_row, again):
        gather.drain()


def sign_step(scale, block_mask, x0):
    row_count, col_count = lax.axis_size("row"), lax.axis_size("col")
    row_lines = (row_count // CORES, CORES)
    outer = math.gcd(col_count, 4)
    col_lines = (outer, col_count // outer)
    rows, cols = x0.shape
    return pl.pallas_call(
        functools.partial(sign_kernel, scale, row_lines, col_lines),
        out_shape=jax.ShapeDtypeStruct(x0.shape, jnp.float32),
        in_specs=[pl.BlockSpec(memory_space=pltpu.SMEM), pl.BlockSpec(memory_space=pltpu.VMEM)],
        out_specs=pl.BlockSpec(memory_space=pltpu.VMEM),
        scratch_shapes=[
            pltpu.VMEM((col_count, rows, cols), jnp.bfloat16),
            pltpu.VMEM((row_count, rows, cols), jnp.bfloat16),
            pltpu.VMEM((row_count, rows, cols), jnp.bfloat16),
            pltpu.VMEM((rows, cols), jnp.float32),
            pltpu.VMEM((rows, cols), jnp.float32),
            *LineGather.semaphores(*col_lines),
            *LineGather.semaphores(*row_lines),
            *LineGather.semaphores(*row_lines),
        ],
        compiler_params=pltpu.CompilerParams(
            vmem_limit_bytes=VMEM_LIMIT, collective_id=0, has_side_effects=True
        ),
        name="sign",
    )(block_mask, x0)


def exchange(blocks, device_count):
    parts = blocks.reshape(device_count, blocks.shape[0] // device_count, HALF, LANES)
    return lax.all_to_all(parts, ("row", "col"), split_axis=0, concat_axis=0, tiled=True).reshape(blocks.shape)


def body(density, core_ham, block_mask, send_blocks, task_atoms, basis, v_loc):
    row_count = lax.axis_size("row")
    device_count = row_count * lax.axis_size("col")
    block_rows = density.shape[0] // EDGE
    local_count = block_rows * (density.shape[1] // EDGE)
    slots = send_blocks[0].reshape(-1)
    index = jnp.where(slots >= 0, slots, local_count)
    atoms = task_atoms[:, 0]
    pair = (atoms[0] * ATOMS + atoms[1]).reshape(-1)
    received = exchange(pick_blocks(index, density), device_count)
    k_slot = grid_step(pair, received, basis[0], v_loc)
    returned = exchange(k_slot, device_count)
    scale = 1.0 / math.sqrt(16.0 * block_rows * row_count)
    ks_matrix, x0 = add_back(scale, index, block_mask, returned, core_ham)
    return (ks_matrix, sign_step(scale, block_mask, x0))


def solution(mesh):
    placed = (
        P("row", "col"),
        P("row", "col"),
        P("row", "col"),
        P(("row", "col"), None, None),
        P(None, ("row", "col"), None, None),
        P(("row", "col"), None, None),
        P(("row", "col"), None),
    )
    return jax.shard_map(
        body,
        mesh=mesh,
        in_specs=placed,
        out_specs=(P("row", "col"), P("row", "col")),
        check_vma=False,
    )
```

time: 274 us -> 183 us (0.67)
  waiting for transfers between devices: 180 us -> 97.7 us
  Pallas kernels: 0 us -> 66.7 us
  matrix products: 32.6 us -> 0 us
  local copies, waits for them, and re-layouts: 26.8 us -> 6.78 us
  between operations: 14 us -> 0.68 us
  other arithmetic: 8.89 us -> 0.56 us
    all_gather x3 -> x0, waiting for transfers between devices: 83.1 us -> none  [the longest x1 52.7 us: body(): left_panel = lax.all_gather(x0, 'col', axis=1, tiled=True)]
    pallas_call x0 -> x4, Pallas kernels: none -> 66.7 us  [the longest x1 39.7 us: sign_step(): pl.pallas_call(functools.partial(sign_kernel, scale, row_lines, col_lines...]
    dot_general x6 -> x0, matrix products: 32.6 us -> none  [the longest x1 10.4 us: body(): lax.dot_general(weighted, basis_vals, (((1,), (1,)), ((), ())), preferred...]
    reshape x7 -> x0, local copies, waits for them, and re-layouts: 10.2 us -> none  [the longest x1 5.66 us: body(): k_pairs = k_all.reshape(ATOMS, block_edge, ATOMS, block_edge).transpose(0...]
    convert_element_type x5 -> x0, other arithmetic: 6.51 us -> none  [the longest x1 3.48 us: body(): jnp.take(k_pairs, pair, axis=0).astype(jnp.bfloat16)]
    unnamed x17 -> x11, local copies, waits for them, and re-layouts: 0.12 us -> 5.96 us
    convert_element_type x3 -> x0, local copies, waits for them, and re-layouts: 5.64 us -> none  [the longest x1 5.47 us: body(): pair_mat = pair_sum.reshape(ATOMS, ATOMS, block_edge, block_edge).transpo...]
    gather x2 -> x0, local copies, waits for them, and re-layouts: 5.03 us -> none  [the longest x1 3.18 us: body(): jnp.take(k_pairs, pair, axis=0).astype(jnp.bfloat16)]
  transfers between devices with their start and end apart: 5 -> 2, of which waited for: 5 -> 2; matrix products, arithmetic and copies ran while one was open for 1% -> 1% of each run, Pallas kernels for 0% -> 0%
where the time goes in v1:
time: 183 us
  waiting for transfers between devices  97.7 us (53%)
  Pallas kernels  66.7 us (36%)
  starting transfers between devices  10.4 us (6%)
  local copies, waits for them, and re-layouts  6.78 us (4%)
    all_to_all x2, waiting for transfers between devices, exchange(): lax.all_to_all(parts, ('row', 'col'), split_axis=0, concat_axis=0, tiled=...  97.7 us
    pallas_call x1, Pallas kernels, sign_step(): pl.pallas_call(functools.partial(sign_kernel, scale, row_lines, col_lines...  39.7 us
    pallas_call x1, Pallas kernels, grid_step(): pl.pallas_call(functools.partial(grid_kernel, chunk), out_shape=jax.Shape...  20.1 us
    all_to_all x2, starting transfers between devices, exchange(): lax.all_to_all(parts, ('row', 'col'), split_axis=0, concat_axis=0, tiled=...  10.4 us
    unnamed x11, local copies, waits for them, and re-layouts  5.96 us
    pallas_call x1, Pallas kernels, add_back(): pl.pallas_call(functools.partial(add_kernel, scale), out_shape=(jax.Shape...  4.02 us
  transfers between devices with their start and end apart: 2, of which 2 were waited for; matrix products, arithmetic and copies ran while one was open for 1% of the time, Pallas kernels for 0%

profile of v1, /device:TPU:1, one launch (start us, length us, event | category | flops | bytes accessed | tf_op | source)
XLA Modules:
  0.0 182.8 jit_solution(8636842169032516341)
XLA Ops:
  0.6 0.8 copy.11
  1.4 0.1 reshape_squeeze.3
  1.5 0.6 compare_select_fusion.index_ref
  2.0 2.9 %pick.1 = bf16[256,32,128]{2,1,0:T(8,128)(2,1)} custom-call(s32[256]{0:T(256)} %compare_select_fusion.index_ref, bf16[512,256]{1,0:T(8,128)(2,1)} %density_ref.1), custom_call_target="tpu_custom_call" | custom-call | tf_op jit(solution)/shard_map/pick/pallas_call | solution.py:58
  4.9 0.0 copy-start.2
  4.9 7.1 %all-to-all-start = ((bf16[32,8,32,128]{3,2,1,0:T(8,128)(2,1)}), bf16[32,8,32,128]{3,2,1,0:T(8,128)(2,1)S(1)}, u32[]{:S(2)}, u32[]{:S(2)}) async-start(bf16[32,8,32,128]{3,2,1,0:T(8,128)(2,1)} %bitcast.10), calls=%async_computation | async-start | bytes 4194304 | tf_op jit(solution)/shard_map/all_to_all | solution.py:371
  12.0 0.0 copy-done.2
  12.0 0.1 copy.12
  12.1 0.7 add.8.pair_ref
  12.8 48.8 %all-to-all-done = bf16[32,8,32,128]{3,2,1,0:T(8,128)(2,1)S(1)} async-done(((bf16[32,8,32,128]{3,2,1,0:T(8,128)(2,1)}), bf16[32,8,32,128]{3,2,1,0:T(8,128)(2,1)S(1)}, u32[]{:S(2)}, u32[]{:S(2)}) %all-to-all-start) | async-done | bytes 2097184 | tf_op jit(solution)/shard_map/all_to_all | solution.py:371
  61.5 0.0 copy-start
  61.5 1.3 copy-done
  62.8 20.1 %grid.1 = bf16[256,32,128]{2,1,0:T(8,128)(2,1)} custom-call(s32[256]{0:T(256)} %add.8.pair_ref, bf16[256,32,128]{2,1,0:T(8,128)(2,1)} %bitcast.7, bf16[1024,2048]{1,0:T(8,128)(2,1)} %bitcast.11, f32[1,2048]{1,0:T(1,128)} %vloc_ref.1), custom_call_target="tpu_custom_call" | custom-call | tf_op jit(solution)/shard_map/grid/pallas_call | solution.py:128
  82.9 0.0 copy-start.3
  82.9 3.3 %all-to-all-start.1 = ((bf16[32,8,32,128]{3,2,1,0:T(8,128)(2,1)}), bf16[32,8,32,128]{3,2,1,0:T(8,128)(2,1)S(1)}, u32[]{:S(2)}, u32[]{:S(2)}) async-start(bf16[32,8,32,128]{3,2,1,0:T(8,128)(2,1)} %bitcast.8), calls=%async_computation.1 | async-start | bytes 4194304 | tf_op jit(solution)/shard_map/all_to_all | solution.py:371
  86.2 0.0 copy-done.3
  86.2 0.7 copy.13.mask_ref
  86.9 49.0 %all-to-all-done.1 = bf16[32,8,32,128]{3,2,1,0:T(8,128)(2,1)S(1)} async-done(((bf16[32,8,32,128]{3,2,1,0:T(8,128)(2,1)}), bf16[32,8,32,128]{3,2,1,0:T(8,128)(2,1)S(1)}, u32[]{:S(2)}, u32[]{:S(2)}) %all-to-all-start.1) | async-done | bytes 2097184 | tf_op jit(solution)/shard_map/all_to_all | solution.py:371
  135.8 0.0 copy-start.1
  135.8 1.3 copy-done.1
  137.2 4.0 %add_back.1 = (f32[512,256]{1,0:T(8,128)}, bf16[512,256]{1,0:T(8,128)(2,1)}) custom-call(s32[256]{0:T(256)} %compare_select_fusion.index_ref, s32[8,4]{1,0:T(8,128)} %copy.13.mask_ref, bf16[256,32,128]{2,1,0:T(8,128)(2,1)} %bitcast.9, f32[512,256]{1,0:T(8,128)} %core_ref.1), custom_call_target="tpu_custom_call" | custom-call | tf_op jit(solution)/shard_map/add_back/pallas_call | solution.py:172
  141.2 39.7 %sign.1 = f32[512,256]{1,0:T(8,128)} custom-call(s32[8,4]{1,0:T(8,128)} %copy.13.mask_ref, bf16[512,256]{1,0:T(8,128)(2,1)} %get-tuple-element.5.x0_ref), custom_call_target="tpu_custom_call" | custom-call | tf_op jit(solution)/shard_map/sign/pallas_call | solution.py:347
  180.9 1.9 %copy.16 = f32[512,256]{1,0:T(8,128)} copy(f32[512,256]{1,0:T(8,128)} %sign.1) | data formatting | bytes 1048576
  (1 shorter events, 0.0 us)
Async XLA Ops:
  4.9 7.1 %copy-start.2 = (s32[2,1,32,8]{2,3,1,0:T(8,128)S(1)}, s32[2,1,32,8]{2,3,1,0:T(8,128)}, u32[]{:S(2)}) copy-start(s32[2,1,32,8]{2,3,1,0:T(8,128)} %param.11) | copy-start | bytes 6148
  4.9 56.6 %all-to-all-start = ((bf16[32,8,32,128]{3,2,1,0:T(8,128)(2,1)}), bf16[32,8,32,128]{3,2,1,0:T(8,128)(2,1)S(1)}, u32[]{:S(2)}, u32[]{:S(2)}) async-start(bf16[32,8,32,128]{3,2,1,0:T(8,128)(2,1)} %bitcast.10), calls=%async_computation | async-start | bytes 4194304 | tf_op jit(solution)/shard_map/all_to_all | solution.py:371
  61.5 1.3 copy-start
  82.9 3.3 %copy-start.3 = (s32[8,4]{0,1:T(4,128)S(1)}, s32[8,4]{0,1:T(4,128)}, u32[]{:S(2)}) copy-start(s32[8,4]{0,1:T(4,128)} %param.9) | copy-start | bytes 388
  82.9 53.0 %all-to-all-start.1 = ((bf16[32,8,32,128]{3,2,1,0:T(8,128)(2,1)}), bf16[32,8,32,128]{3,2,1,0:T(8,128)(2,1)S(1)}, u32[]{:S(2)}, u32[]{:S(2)}) async-start(bf16[32,8,32,128]{3,2,1,0:T(8,128)(2,1)} %bitcast.8), calls=%async_computation.1 | async-start | bytes 4194304 | tf_op jit(solution)/shard_map/all_to_all | solution.py:371
  135.8 1.3 copy-start.1

commit v2 on v1

--- a/solution.py
+++ b/solution.py
@@ -32,38 +32,323 @@
     return join_pair(top, bottom)
 
 
-def pick_kernel(index_ref, density_ref, out_ref, packed):
+class Plane:
+    def __init__(self, outer, inner, row_count):
+        self.outer, self.inner, self.count = outer, inner, row_count * inner
+        self.row, col = lax.axis_index("row"), lax.axis_index("col")
+        self.a, self.b = col // inner, col % inner
+        self.place = self.row * inner + self.b
+
+    def peer(self, offset):
+        return lax.rem(self.place + 1 + offset, self.count)
+
+    def device(self, place):
+        return (place // self.inner, self.a * self.inner + place % self.inner)
+
+    def owner(self, place, outer_at):
+        return (place // self.inner) * (self.outer * self.inner) + outer_at * self.inner + place % self.inner
+
+    def on_line(self, outer_at):
+        return (self.row, outer_at * self.inner + self.b)
+
+    def greet(self, line):
+        barrier = pltpu.get_barrier_semaphore()
+
+        def signal(offset, carry):
+            pl.semaphore_signal(barrier, inc=1, device_id=self.device(self.peer(offset)), device_id_type=MESH)
+            return carry
+
+        lax.fori_loop(0, self.count - 1, signal, 0)
+        greet([line], self.count - 1)
+
+
+def send_kernel(
+    outer, inner, row_count, index_ref, lists_ref, density_ref, out_ref, kept_ref,
+    own, lists, lists_smem, stage, list_sem, recv_sem, send_sem, tile_send, tile_recv, *rest
+):
+    plane = Plane(outer, inner, row_count)
+    a = plane.a
     rows, cols = density_ref.shape
     across = cols // EDGE
     count = (rows // EDGE) * across
-    packed[count] = jnp.zeros((HALF, LANES), packed.dtype)
+    slots = stage.shape[2]
+    entries = LineGather(lists.at.__getitem__, outer, 1, a, plane.on_line, rest[0:3])
+    arrived = (rest[3 : 2 + outer], rest[2 + outer :])
+    for tile in (own, *arrived[0], *arrived[1]):
+        tile[count] = jnp.zeros((HALF, LANES), tile.dtype)
+    plane.greet(entries)
+    lists[a] = lists_ref[...]
     for i in range(rows // EDGE):
         for j in range(0, across, 2):
             lanes = slice(j * EDGE, (j + 2) * EDGE)
             top = density_ref[i * EDGE : i * EDGE + HALF, lanes].astype(jnp.float32)
             bottom = density_ref[i * EDGE + HALF : (i + 1) * EDGE, lanes].astype(jnp.float32)
             first, second = split_pair(top, bottom)
-            packed[i * across + j] = first.astype(packed.dtype)
-            packed[i * across + j + 1] = second.astype(packed.dtype)
-
-    def copy_slot(slot, carry):
-        out_ref[slot] = packed[index_ref[slot]]
-        return carry
-
-    lax.fori_loop(0, out_ref.shape[0], copy_slot, 0, unroll=8)
-
-
-def pick_blocks(index, density):
+            own[i * across + j] = first.astype(own.dtype)
+            own[i * across + j + 1] = second.astype(own.dtype)
+
+    def passes(d, step):
+        source, target = a - d * step, a + step
+        return jnp.logical_and(
+            jnp.logical_and(source >= 0, source < outer), jnp.logical_and(target >= 0, target < outer)
+        )
+
+    def pass_on(d, way, step):
+        tile = arrived[way][d - 1] if d else own
+        return pltpu.make_async_remote_copy(
+            src_ref=tile.at[pl.ds(0, count)],
+            dst_ref=arrived[way][d].at[pl.ds(0, count)],
+            send_sem=tile_send.at[way, d],
+            recv_sem=tile_recv.at[way, d],
+            device_id=plane.on_line(a + step),
+            device_id_type=MESH,
+        )
+
+    def serve(tile, source, number):
+        def pick(offset, place):
+            for slot in range(slots):
+                stage[source, offset, slot] = tile[number(place * slots + slot)]
+
+        def one(offset, carry):
+            place = plane.peer(offset)
+            pick(offset, place)
+            pltpu.make_async_remote_copy(
+                src_ref=stage.at[source, offset],
+                dst_ref=out_ref.at[plane.owner(plane.place, source)],
+                send_sem=send_sem,
+                recv_sem=recv_sem,
+                device_id=plane.device(place),
+                device_id_type=MESH,
+            ).start()
+            return carry
+
+        lax.fori_loop(0, plane.count - 1, one, 0)
+        pick(plane.count - 1, plane.place)
+        pltpu.make_async_copy(
+            stage.at[source, plane.count - 1], out_ref.at[plane.owner(plane.place, source)], recv_sem
+        ).start()
+
+    entry_steps = entries.steps()
+    for d in range(outer):
+        next(entry_steps)
+        if d:
+            for way, step in enumerate((1, -1)):
+
+                @pl.when(jnp.logical_and(a - d * step >= 0, a - d * step < outer))
+                def _():
+                    tile = arrived[way][d - 1].at[pl.ds(0, count)]
+                    pltpu.make_async_copy(tile, tile, tile_recv.at[way, d - 1]).wait()
+
+        if d < outer - 1:
+            for way, step in enumerate((1, -1)):
+
+                @pl.when(passes(d, step))
+                def _():
+                    pass_on(d, way, step).start()
+
+        if d == 0:
+            serve(own, a, lambda at: index_ref[a, at])
+            continue
+        for way, step in enumerate((1, -1)):
+            source = a - d * step
+
+            @pl.when(jnp.logical_and(source >= 0, source < outer))
+            def _():
+                copy = pltpu.make_async_copy(lists.at[source], lists_smem.at[source], list_sem)
+                copy.start()
+                copy.wait()
+                serve(arrived[way][d - 1], source, lambda at: lists_smem[source, a, at])
+
+    kept_ref[...] = jnp.zeros_like(kept_ref)
+    for i in range(outer):
+        kept_ref[i : i + 1, :] = lists[i, pl.ds(a, 1), :]
+    for d in range(outer - 1):
+        for way, step in enumerate((1, -1)):
+
+            @pl.when(passes(d, step))
+            def _():
+                pass_on(d, way, step).wait_send()
+
+    entries.drain()
+    sent = stage.at[:, pl.ds(0, plane.count - 1)]
+    pltpu.make_async_copy(sent, sent, send_sem).wait()
+    pltpu.make_async_copy(out_ref, out_ref, recv_sem).wait()
+
+
+def send_blocks_out(lines, slots, lists, density):
+    outer, inner = lines
+    row_count, col_count = lax.axis_size("row"), lax.axis_size("col")
+    plane_count = row_count * inner
     count = (density.shape[0] // EDGE) * (density.shape[1] // EDGE)
+    vmem = pl.BlockSpec(memory_space=pltpu.VMEM)
     return pl.pallas_call(
-        pick_kernel,
-        out_shape=jax.ShapeDtypeStruct((index.shape[0], HALF, LANES), jnp.bfloat16),
-        in_specs=[pl.BlockSpec(memory_space=pltpu.SMEM), pl.BlockSpec(memory_space=pltpu.VMEM)],
-        out_specs=pl.BlockSpec(memory_space=pltpu.VMEM),
-        scratch_shapes=[pltpu.VMEM((count + 1, HALF, LANES), jnp.bfloat16)],
-        compiler_params=pltpu.CompilerParams(vmem_limit_bytes=VMEM_LIMIT),
-        name="pick",
-    )(index, density)
+        functools.partial(send_kernel, outer, inner, row_count),
+        out_shape=(
+            jax.ShapeDtypeStruct((row_count * col_count, slots, HALF, LANES), jnp.bfloat16),
+            jax.ShapeDtypeStruct(lists.shape, jnp.int32),
+        ),
+        in_specs=[pl.BlockSpec(memory_space=pltpu.SMEM), vmem, vmem],
+        out_specs=(pl.BlockSpec(memory_space=pl.ANY), vmem),
+        scratch_shapes=[
+            pltpu.VMEM((count + 1, HALF, LANES), jnp.bfloat16),
+            pltpu.VMEM((outer, *lists.shape), jnp.int32),
+            pltpu.SMEM((outer, *lists.shape), jnp.int32),
+            pltpu.VMEM((outer, plane_count, slots, HALF, LANES), jnp.bfloat16),
+            pltpu.SemaphoreType.DMA,
+            pltpu.SemaphoreType.DMA,
+            pltpu.SemaphoreType.DMA,
+            pltpu.SemaphoreType.DMA((2, outer)),
+            pltpu.SemaphoreType.DMA((2, outer)),
+            *LineGather.semaphores(outer, 1),
+            *[pltpu.VMEM((count + 1, HALF, LANES), jnp.bfloat16)] * (2 * (outer - 1)),
+        ],
+        compiler_params=pltpu.CompilerParams(
+            vmem_limit_bytes=VMEM_LIMIT, collective_id=1, has_side_effects=True
+        ),
+        name="send_out",
+    )(lists, lists, density)
+
+
+def back_kernel(
+    outer, inner, row_count, kept_ref, slots_ref, out_ref,
+    landed, wide, total, sums, arriving, land_sem, send_sem, line_send, line_recv
+):
+    plane = Plane(outer, inner, row_count)
+    a, b = plane.a, plane.b
+    count = out_ref.shape[0]
+    slots = slots_ref.shape[1]
+    terms = plane.count * slots
+    line = LineGather(None, outer, 1, a, plane.on_line, (None,) * 3)
+    plane.greet(line)
+
+    def send_plane(target):
+        def one(offset, carry):
+            place = plane.peer(offset)
+            pltpu.make_async_remote_copy(
+                src_ref=slots_ref.at[plane.owner(place, target)],
+                dst_ref=landed.at[target, plane.place],
+                send_sem=send_sem,
+                recv_sem=land_sem.at[target],
+                device_id=plane.device(place),
+                device_id_type=MESH,
+            ).start()
+            return carry
+
+        lax.fori_loop(0, plane.count - 1, one, 0)
+        pltpu.make_async_copy(
+            slots_ref.at[plane.owner(plane.place, target)], landed.at[target, plane.place], land_sem.at[target]
+        ).start()
+
+    def combine(target):
+        pltpu.make_async_copy(landed.at[target], landed.at[target], land_sem.at[target]).wait()
+        wide[...] = landed[target].astype(jnp.float32).reshape(wide.shape)
+        numbers = lax.broadcasted_iota(jnp.int32, (count, terms), 0)
+        chosen = jnp.where(numbers == kept_ref[pl.ds(target, 1), 0:terms], 1.0, 0.0).astype(jnp.bfloat16)
+        for line_at in range(HALF):
+            part = wide[pl.ds(line_at, terms, stride=HALF), :].astype(jnp.bfloat16)
+            total[pl.ds(line_at, count, stride=HALF), :] = jnp.dot(
+                chosen, part, preferred_element_type=jnp.float32
+            )
+
+    def wait_line(target, side):
+        ref = arriving.at[target, side]
+        pltpu.make_async_copy(ref, ref, line_recv.at[target, side]).wait()
+
+    def pass_on(target, step, side):
+        return pltpu.make_async_remote_copy(
+            src_ref=sums.at[target],
+            dst_ref=arriving.at[target, side],
+            send_sem=line_send.at[target],
+            recv_sem=line_recv.at[target, side],
+            device_id=plane.on_line(a + step),
+            device_id_type=MESH,
+        )
+
+    order = [(d, step) for d in range(outer - 1, 0, -1) for step in (1, -1)] + [(0, 1)]
+
+    def each(d, step, act):
+        target = a + d * step
+
+        @pl.when(jnp.logical_and(target >= 0, target < outer))
+        def _():
+            act(target)
+
+    def nth(k, act):
+        far = jnp.maximum(a, outer - 1 - a)
+        near = outer - 1 - far
+        up = a < outer - 1 - a
+        long = far - near
+        alone = jnp.where(up, a + far - k, a - far + k)
+        rest = k - long
+        dist = near - rest // 2
+        paired = jnp.where(lax.rem(rest, 2) == 0, a + dist, a - dist)
+        act(jnp.where(rest < 0, alone, paired))
+
+    nth(0, send_plane)
+    if outer > 1:
+        nth(1, send_plane)
+    for k in range(outer):
+
+        def handle(target):
+            combine(target)
+            for side, step in ((0, 1), (1, -1)):
+
+                @pl.when((target - a) * step > 0)
+                def _():
+                    @pl.when(jnp.logical_and(a - step >= 0, a - step < outer))
+                    def _():
+                        wait_line(target, side)
+                        total[...] += arriving[target, side].astype(jnp.float32).reshape(total.shape)
+
+                    sums[target] = total[...].astype(jnp.bfloat16).reshape(sums.shape[1:])
+                    pass_on(target, step, side).start()
+
+        nth(k, handle)
+        if k + 2 < outer:
+            nth(k + 2, send_plane)
+    for side, step in ((0, 1), (1, -1)):
+
+        @pl.when(jnp.logical_and(a - step >= 0, a - step < outer))
+        def _():
+            wait_line(a, side)
+            total[...] += arriving[a, side].astype(jnp.float32).reshape(total.shape)
+
+    out_ref[...] = total[...].reshape(out_ref.shape)
+    for d, step in order:
+        if d:
+            side = 0 if step > 0 else 1
+            each(d, step, lambda target: pass_on(target, step, side).wait_send())
+    sent = landed.at[:, pl.ds(0, plane.count - 1)]
+    pltpu.make_async_copy(sent, sent, send_sem).wait()
+
+
+def send_blocks_back(lines, count, kept, blocks):
+    outer, inner = lines
+    row_count = lax.axis_size("row")
+    plane_count = row_count * inner
+    slots = blocks.shape[1]
+    vmem = pl.BlockSpec(memory_space=pltpu.VMEM)
+    return pl.pallas_call(
+        functools.partial(back_kernel, outer, inner, row_count),
+        out_shape=jax.ShapeDtypeStruct((count, HALF, LANES), jnp.float32),
+        in_specs=[vmem, pl.BlockSpec(memory_space=pl.ANY)],
+        out_specs=vmem,
+        scratch_shapes=[
+            pltpu.VMEM((outer, plane_count, slots, HALF, LANES), jnp.bfloat16),
+            pltpu.VMEM((plane_count * slots * HALF, LANES), jnp.float32),
+            pltpu.VMEM((count * HALF, LANES), jnp.float32),
+            pltpu.VMEM((outer, count, HALF, LANES), jnp.bfloat16),
+            pltpu.VMEM((outer, 2, count, HALF, LANES), jnp.bfloat16),
+            pltpu.SemaphoreType.DMA((outer,)),
+            pltpu.SemaphoreType.DMA,
+            pltpu.SemaphoreType.DMA((outer,)),
+            pltpu.SemaphoreType.DMA((outer, 2)),
+        ],
+        compiler_params=pltpu.CompilerParams(
+            vmem_limit_bytes=VMEM_LIMIT, collective_id=2, has_side_effects=True
+        ),
+        name="send_back",
+    )(kept, blocks)
 
 
 def grid_kernel(chunk, pair_ref, recv_ref, basis_ref, vloc_ref, out_ref, sums, pair_mat, k_all):
@@ -145,17 +430,9 @@
     return jnp.where(low, mask_ref[i, j].astype(jnp.float32), mask_ref[i, j + 1].astype(jnp.float32))
 
 
-def add_kernel(scale, index_ref, mask_ref, back_ref, core_ref, ks_ref, x0_ref, sums):
+def add_kernel(scale, mask_ref, sums, core_ref, ks_ref, x0_ref):
     rows, cols = core_ref.shape
     across = cols // EDGE
-    sums[...] = jnp.zeros_like(sums)
-
-    def add_slot(slot, carry):
-        at = index_ref[slot]
-        sums[at] = sums[at] + back_ref[slot].astype(jnp.float32)
-        return carry
-
-    lax.fori_loop(0, back_ref.shape[0], add_slot, 0, unroll=8)
     for i in range(rows // EDGE):
         for j in range(0, across, 2):
             lanes = slice(j * EDGE, (j + 2) * EDGE)
@@ -167,25 +444,23 @@
             x0_ref[high:low, lanes] = kept.astype(jnp.bfloat16)
 
 
-def add_back(scale, index, block_mask, returned, core_ham):
-    count = (core_ham.shape[0] // EDGE) * (core_ham.shape[1] // EDGE)
+def add_back(scale, block_mask, sums, core_ham):
     return pl.pallas_call(
         functools.partial(add_kernel, scale),
         out_shape=(
             jax.ShapeDtypeStruct(core_ham.shape, jnp.float32),
             jax.ShapeDtypeStruct(core_ham.shape, jnp.bfloat16),
         ),
-        in_specs=[pl.BlockSpec(memory_space=pltpu.SMEM)] * 2 + [pl.BlockSpec(memory_space=pltpu.VMEM)] * 2,
+        in_specs=[pl.BlockSpec(memory_space=pltpu.SMEM)] + [pl.BlockSpec(memory_space=pltpu.VMEM)] * 2,
         out_specs=(pl.BlockSpec(memory_space=pltpu.VMEM),) * 2,
-        scratch_shapes=[pltpu.VMEM((count + 1, HALF, LANES), jnp.float32)],
         compiler_params=pltpu.CompilerParams(vmem_limit_bytes=VMEM_LIMIT),
         name="add_back",
-    )(index, block_mask, returned, core_ham)
+    )(block_mask, sums, core_ham)
 
 
 class LineGather:
-    def __init__(self, held, outer, inner, place, device_at, sems):
-        self.held, self.outer, self.inner = held, outer, inner
+    def __init__(self, piece, outer, inner, place, device_at, sems):
+        self.piece, self.outer, self.inner = piece, outer, inner
         self.a, self.b = place // inner, place % inner
         self.device_at = device_at
         self.out_sem, self.in_sem, self.recv_sem = sems
@@ -203,8 +478,8 @@
     def send(self, cond, source, target, sem):
         def describe():
             return pltpu.make_async_remote_copy(
-                src_ref=self.held.at[source],
-                dst_ref=self.held.at[source],
+                src_ref=self.piece(source),
+                dst_ref=self.piece(source),
                 send_sem=sem,
                 recv_sem=self.recv_sem.at[source],
                 device_id=self.device_at(target),
@@ -218,7 +493,7 @@
         self.sent.append((cond, describe))
 
     def arrive(self, source):
-        pltpu.make_async_copy(self.held.at[source], self.held.at[source], self.recv_sem.at[source]).wait()
+        pltpu.make_async_copy(self.piece(source), self.piece(source), self.recv_sem.at[source]).wait()
 
     def along_inner(self, cond, outer_at, inner_from, step, sem):
         target = self.b + step
@@ -285,9 +560,9 @@
         ]
 
 
-def greet(gathers):
+def greet(gathers, others=0):
     barrier = pltpu.get_barrier_semaphore()
-    count = 0
+    count = others
     for gather in gathers:
         for cond, a, b in gather.neighbours():
 
@@ -319,9 +594,9 @@
 def sign_kernel(scale, row_lines, col_lines, mask_ref, x0_ref, out_ref, left, right, second, mask, acc, *sems):
     row, col = lax.axis_index("row"), lax.axis_index("col")
     rows, cols = x0_ref.shape
-    along_col = LineGather(left, *col_lines, col, lambda at: (row, at), sems[0:3])
-    along_row = LineGather(right, *row_lines, row, lambda at: (at, col), sems[3:6])
-    again = LineGather(second, *row_lines, row, lambda at: (at, col), sems[6:9])
+    along_col = LineGather(left.at.__getitem__, *col_lines, col, lambda at: (row, at), sems[0:3])
+    along_row = LineGather(right.at.__getitem__, *row_lines, row, lambda at: (at, col), sems[3:6])
+    again = LineGather(second.at.__getitem__, *row_lines, row, lambda at: (at, col), sems[6:9])
     greet([along_col, along_row])
     left[col] = x0_ref[...]
     right[row] = x0_ref[...]
@@ -366,25 +641,23 @@
     )(block_mask, x0)
 
 
-def exchange(blocks, device_count):
-    parts = blocks.reshape(device_count, blocks.shape[0] // device_count, HALF, LANES)
-    return lax.all_to_all(parts, ("row", "col"), split_axis=0, concat_axis=0, tiled=True).reshape(blocks.shape)
-
-
 def body(density, core_ham, block_mask, send_blocks, task_atoms, basis, v_loc):
-    row_count = lax.axis_size("row")
-    device_count = row_count * lax.axis_size("col")
+    row_count, col_count = lax.axis_size("row"), lax.axis_size("col")
     block_rows = density.shape[0] // EDGE
     local_count = block_rows * (density.shape[1] // EDGE)
-    slots = send_blocks[0].reshape(-1)
-    index = jnp.where(slots >= 0, slots, local_count)
+    capacity = send_blocks.shape[2]
+    outer = math.gcd(col_count, 4)
+    inner = col_count // outer
+    slots = send_blocks[0].reshape(row_count, outer, inner * capacity)
+    lists = jnp.where(slots >= 0, slots, local_count).transpose(1, 0, 2).reshape(outer, -1)
+    lists = jnp.pad(lists, ((0, -outer % 8), (0, -lists.shape[1] % 128)))
     atoms = task_atoms[:, 0]
     pair = (atoms[0] * ATOMS + atoms[1]).reshape(-1)
-    received = exchange(pick_blocks(index, density), device_count)
-    k_slot = grid_step(pair, received, basis[0], v_loc)
-    returned = exchange(k_slot, device_count)
+    received, kept = send_blocks_out((outer, inner), capacity, lists, density)
+    k_slot = grid_step(pair, received.reshape(-1, HALF, LANES), basis[0], v_loc)
+    sums = send_blocks_back((outer, inner), local_count, kept, k_slot.reshape(received.shape))
     scale = 1.0 / math.sqrt(16.0 * block_rows * row_count)
-    ks_matrix, x0 = add_back(scale, index, block_mask, returned, core_ham)
+    ks_matrix, x0 = add_back(scale, block_mask, sums, core_ham)
     return (ks_matrix, sign_step(scale, block_mask, x0))
 
 

time: 183 us -> 138 us (0.75)
  waiting for transfers between devices: 97.7 us -> 0 us
  Pallas kernels: 66.7 us -> 131 us
  starting transfers between devices: 10.4 us -> 0 us
  local copies, waits for them, and re-layouts: 6.78 us -> 4.81 us
    all_to_all x2 -> x0, waiting for transfers between devices: 97.7 us -> none  [exchange(): lax.all_to_all(parts, ('row', 'col'), split_axis=0, concat_axis=0, tiled=...]
    pallas_call x1 -> x2, Pallas kernels: 2.87 us -> 69.3 us  [the longest x1 34.8 us: send_blocks_back(): pl.pallas_call(functools.partial(back_kernel, outer, inner, row_count), o...]
    all_to_all x2 -> x0, starting transfers between devices: 10.4 us -> none  [exchange(): lax.all_to_all(parts, ('row', 'col'), split_axis=0, concat_axis=0, tiled=...]
    unnamed x11 -> x5, local copies, waits for them, and re-layouts: 5.96 us -> 3.31 us
  transfers between devices with their start and end apart: 2 -> 0, of which waited for: 2 -> 0; matrix products, arithmetic and copies ran while one was open for 1% -> 0% of each run, Pallas kernels for 0% -> 0%
where the time goes in v2:
time: 138 us
  Pallas kernels  131 us (95%)
  local copies, waits for them, and re-layouts  4.81 us (3%)
    pallas_call x1, Pallas kernels, sign_step(): pl.pallas_call(functools.partial(sign_kernel, scale, row_lines, col_lines...  39.7 us
    pallas_call x1, Pallas kernels, send_blocks_back(): pl.pallas_call(functools.partial(back_kernel, outer, inner, row_count), o...  34.8 us
    pallas_call x1, Pallas kernels, send_blocks_out(): pl.pallas_call(functools.partial(send_kernel, outer, inner, row_count), o...  34.5 us
    pallas_call x1, Pallas kernels, grid_step(): pl.pallas_call(functools.partial(grid_kernel, chunk), out_shape=jax.Shape...  20.1 us
    unnamed x5, local copies, waits for them, and re-layouts  3.31 us

profile of v2, /device:TPU:1, one launch (start us, length us, event | category | flops | bytes accessed | tf_op | source)
XLA Modules:
  0.0 137.6 jit_solution(3729273607997249952)
XLA Ops:
  0.6 0.8 copy.11
  1.4 0.1 reshape_squeeze.3
  1.5 0.1 reshape.23
  1.6 0.6 pad.4.index_ref.lists_ref
  2.2 34.5 %send_out.1 = (bf16[32,8,32,128]{3,2,1,0:T(8,128)(2,1)}, s32[8,128]{1,0:T(8,128)}) custom-call(s32[8,128]{1,0:T(8,128)} %pad.4.index_ref.lists_ref, s32[8,128]{1,0:T(8,128)} %pad.4.index_ref.lists_ref, bf16[512,256]{1,0:T(8,128)(2,1)} %density_ref.1), custom_call_target="tpu_custom_call" | custom-call | tf_op jit(solution)/shard_map/send_out/pallas_call | solution.py:184
  36.7 0.7 slice_add_fusion
  37.4 0.1 copy.13
  37.5 0.7 add.10.pair_ref
  38.1 20.1 %grid.1 = bf16[256,32,128]{2,1,0:T(8,128)(2,1)} custom-call(s32[256]{0:T(256)} %add.10.pair_ref, bf16[256,32,128]{2,1,0:T(8,128)(2,1)} %bitcast.9, bf16[1024,2048]{1,0:T(8,128)(2,1)} %bitcast.8, f32[1,2048]{1,0:T(1,128)} %vloc_ref.1), custom_call_target="tpu_custom_call" | custom-call | tf_op jit(solution)/shard_map/grid/pallas_call | solution.py:413
  58.2 0.0 copy-start
  58.2 34.8 %send_back.1.sums = f32[32,32,128]{2,1,0:T(8,128)} custom-call(s32[8,128]{1,0:T(8,128)} %get-tuple-element.6.kept_ref, bf16[32,8,32,128]{3,2,1,0:T(8,128)(2,1)} %bitcast.7), custom_call_target="tpu_custom_call" | custom-call | tf_op jit(solution)/shard_map/send_back/pallas_call | solution.py:331
  93.0 0.0 copy-done
  93.0 0.7 copy.14.mask_ref
  93.7 2.3 %add_back.1 = (f32[512,256]{1,0:T(8,128)}, bf16[512,256]{1,0:T(8,128)(2,1)}) custom-call(s32[8,4]{1,0:T(8,128)} %copy.14.mask_ref, f32[32,32,128]{2,1,0:T(8,128)} %send_back.1.sums, f32[512,256]{1,0:T(8,128)} %core_ref.1), custom_call_target="tpu_custom_call" | custom-call | tf_op jit(solution)/shard_map/add_back/pallas_call | solution.py:448
  96.0 39.7 %sign.1 = f32[512,256]{1,0:T(8,128)} custom-call(s32[8,4]{1,0:T(8,128)} %copy.14.mask_ref, bf16[512,256]{1,0:T(8,128)(2,1)} %get-tuple-element.9.x0_ref), custom_call_target="tpu_custom_call" | custom-call | tf_op jit(solution)/shard_map/sign/pallas_call | solution.py:622
  135.7 1.9 %copy.17 = f32[512,256]{1,0:T(8,128)} copy(f32[512,256]{1,0:T(8,128)} %sign.1) | data formatting | bytes 1048576
  (2 shorter events, 0.0 us)
Async XLA Ops:
  58.2 34.8 %copy-start = (s32[8,4]{0,1:T(4,128)S(1)}, s32[8,4]{0,1:T(4,128)}, u32[]{:S(2)}) copy-start(s32[8,4]{0,1:T(4,128)} %param.9) | copy-start | bytes 388

commit v3 on v2

--- a/solution.py
+++ b/solution.py
@@ -210,12 +210,14 @@
 
 
 def back_kernel(
-    outer, inner, row_count, kept_ref, slots_ref, out_ref,
-    landed, wide, total, sums, arriving, land_sem, send_sem, line_send, line_recv
+    scale, outer, inner, row_count, kept_ref, mask_ref, slots_ref, core_ref, ham_ref, x0_ref, x3_ref,
+    landed, wide, total, sums, arriving, land_sem, send_sem, line_send, line_recv, *rest
 ):
     plane = Plane(outer, inner, row_count)
     a, b = plane.a, plane.b
-    count = out_ref.shape[0]
+    rows, cols = core_ref.shape
+    across = cols // EDGE
+    count = sums.shape[1]
     slots = slots_ref.shape[1]
     terms = plane.count * slots
     line = LineGather(None, outer, 1, a, plane.on_line, (None,) * 3)
@@ -227,7 +229,7 @@
             pltpu.make_async_remote_copy(
                 src_ref=slots_ref.at[plane.owner(place, target)],
                 dst_ref=landed.at[target, plane.place],
-                send_sem=send_sem,
+                send_sem=send_sem.at[target],
                 recv_sem=land_sem.at[target],
                 device_id=plane.device(place),
                 device_id_type=MESH,
@@ -284,10 +286,15 @@
         paired = jnp.where(lax.rem(rest, 2) == 0, a + dist, a - dist)
         act(jnp.where(rest < 0, alone, paired))
 
+    def sent_plane(target):
+        sent = landed.at[target, pl.ds(0, plane.count - 1)]
+        pltpu.make_async_copy(sent, sent, send_sem.at[target]).wait()
+
     nth(0, send_plane)
-    if outer > 1:
-        nth(1, send_plane)
     for k in range(outer):
+        nth(k, sent_plane)
+        if k + 1 < outer:
+            nth(k + 1, send_plane)
 
         def handle(target):
             combine(target)
@@ -304,8 +311,6 @@
                     pass_on(target, step, side).start()
 
         nth(k, handle)
-        if k + 2 < outer:
-            nth(k + 2, send_plane)
     for side, step in ((0, 1), (1, -1)):
 
         @pl.when(jnp.logical_and(a - step >= 0, a - step < outer))
@@ -313,26 +318,42 @@
             wait_line(a, side)
             total[...] += arriving[a, side].astype(jnp.float32).reshape(total.shape)
 
-    out_ref[...] = total[...].reshape(out_ref.shape)
+    for i in range(rows // EDGE):
+        for j in range(0, across, 2):
+            lanes = slice(j * EDGE, (j + 2) * EDGE)
+            high, mid, low = i * EDGE, i * EDGE + HALF, (i + 1) * EDGE
+            at = (i * across + j) * HALF
+            top, bottom = join_pair(total[at : at + HALF, :], total[at + HALF : at + 2 * HALF, :])
+            ham_ref[high:mid, lanes] = top
+            ham_ref[mid:low, lanes] = bottom
+            ks = core_ref[high:low, lanes] + ham_ref[high:low, lanes]
+            x0_ref[high:low, lanes] = (block_masks(mask_ref, i, j) * ks * scale).astype(jnp.bfloat16)
+
+    sign_part(plane, mask_ref, x0_ref, x3_ref, *rest)
     for d, step in order:
         if d:
             side = 0 if step > 0 else 1
             each(d, step, lambda target: pass_on(target, step, side).wait_send())
-    sent = landed.at[:, pl.ds(0, plane.count - 1)]
-    pltpu.make_async_copy(sent, sent, send_sem).wait()
-
-
-def send_blocks_back(lines, count, kept, blocks):
+
+
+def send_blocks_back(scale, lines, kept, blocks, block_mask, core_ham):
     outer, inner = lines
-    row_count = lax.axis_size("row")
+    row_count, col_count = lax.axis_size("row"), lax.axis_size("col")
+    row_lines = (row_count // CORES, CORES)
     plane_count = row_count * inner
     slots = blocks.shape[1]
+    rows, cols = core_ham.shape
+    count = (rows // EDGE) * (cols // EDGE)
     vmem = pl.BlockSpec(memory_space=pltpu.VMEM)
     return pl.pallas_call(
-        functools.partial(back_kernel, outer, inner, row_count),
-        out_shape=jax.ShapeDtypeStruct((count, HALF, LANES), jnp.float32),
-        in_specs=[vmem, pl.BlockSpec(memory_space=pl.ANY)],
-        out_specs=vmem,
+        functools.partial(back_kernel, scale, outer, inner, row_count),
+        out_shape=(
+            jax.ShapeDtypeStruct(core_ham.shape, jnp.float32),
+            jax.ShapeDtypeStruct(core_ham.shape, jnp.bfloat16),
+            jax.ShapeDtypeStruct(core_ham.shape, jnp.float32),
+        ),
+        in_specs=[vmem, vmem, pl.BlockSpec(memory_space=pl.ANY), vmem],
+        out_specs=(vmem,) * 3,
         scratch_shapes=[
             pltpu.VMEM((outer, plane_count, slots, HALF, LANES), jnp.bfloat16),
             pltpu.VMEM((plane_count * slots * HALF, LANES), jnp.float32),
@@ -340,21 +361,33 @@
             pltpu.VMEM((outer, count, HALF, LANES), jnp.bfloat16),
             pltpu.VMEM((outer, 2, count, HALF, LANES), jnp.bfloat16),
             pltpu.SemaphoreType.DMA((outer,)),
-            pltpu.SemaphoreType.DMA,
+            pltpu.SemaphoreType.DMA((outer,)),
             pltpu.SemaphoreType.DMA((outer,)),
             pltpu.SemaphoreType.DMA((outer, 2)),
+            pltpu.VMEM((col_count, rows, cols), jnp.bfloat16),
+            pltpu.VMEM((row_count, rows, cols), jnp.bfloat16),
+            pltpu.VMEM((row_count, rows, cols), jnp.bfloat16),
+            pltpu.VMEM((rows, cols), jnp.float32),
+            pltpu.VMEM((rows, cols), jnp.float32),
+            *LineGather.semaphores(outer, inner),
+            *LineGather.semaphores(inner, outer),
+            *LineGather.semaphores(*row_lines),
+            *LineGather.semaphores(*row_lines),
         ],
         compiler_params=pltpu.CompilerParams(
             vmem_limit_bytes=VMEM_LIMIT, collective_id=2, has_side_effects=True
         ),
-        name="send_back",
-    )(kept, blocks)
-
-
-def grid_kernel(chunk, pair_ref, recv_ref, basis_ref, vloc_ref, out_ref, sums, pair_mat, k_all):
+        name="back_and_sign",
+    )(kept, block_mask, blocks, core_ham)
+
+
+def grid_kernel(
+    chunk, pair_ref, recv_ref, basis_hbm, vloc_ref, out_ref, sums, pair_mat, k_all, basis_ref, weighted, sem
+):
     cells = basis_ref.shape[1]
+    load = pltpu.make_async_copy(basis_hbm, basis_ref, sem)
+    load.start()
     sums[...] = jnp.zeros_like(sums)
-    k_all[...] = jnp.zeros_like(k_all)
 
     def add_slot(slot, carry):
         at = pair_ref[slot]
@@ -373,6 +406,7 @@
         return carry
 
     lax.fori_loop(0, ATOMS, assemble, 0)
+    load.wait()
 
     def integrate(step, carry):
         at = pl.ds(pl.multiple_of(step * chunk, chunk), chunk)
@@ -381,13 +415,20 @@
         wide = vals.astype(jnp.float32)
         rho = jnp.sum(wide * mixed, axis=0, keepdims=True)
         pot = vloc_ref[:, at] + 0.5 * rho / jnp.sqrt(1.0 + rho * rho)
-        weighted = (wide * pot).astype(jnp.bfloat16)
-        k_all[...] += lax.dot_general(
-            weighted, vals, (((1,), (1,)), ((), ())), preferred_element_type=jnp.float32
+        weighted[:, at] = (wide * pot).astype(jnp.bfloat16)
+        return carry
+
+    lax.fori_loop(0, cells // chunk, integrate, 0)
+    columns = 4 * EDGE
+
+    def multiply(step, carry):
+        at = pl.ds(pl.multiple_of(step * columns, columns), columns)
+        k_all[:, at] = lax.dot_general(
+            weighted[...], basis_ref[at, :], (((1,), (1,)), ((), ())), preferred_element_type=jnp.float32
         )
         return carry
 
-    lax.fori_loop(0, cells // chunk, integrate, 0)
+    lax.fori_loop(0, k_all.shape[1] // columns, multiply, 0)
 
     def split(a, carry):
         row = pl.multiple_of(a * EDGE, EDGE)
@@ -413,12 +454,20 @@
     return pl.pallas_call(
         functools.partial(grid_kernel, chunk),
         out_shape=jax.ShapeDtypeStruct(received.shape, jnp.bfloat16),
-        in_specs=[pl.BlockSpec(memory_space=pltpu.SMEM)] + [pl.BlockSpec(memory_space=pltpu.VMEM)] * 3,
+        in_specs=[
+            pl.BlockSpec(memory_space=pltpu.SMEM),
+            pl.BlockSpec(memory_space=pltpu.VMEM),
+            pl.BlockSpec(memory_space=pl.ANY),
+            pl.BlockSpec(memory_space=pltpu.VMEM),
+        ],
         out_specs=pl.BlockSpec(memory_space=pltpu.VMEM),
         scratch_shapes=[
             pltpu.VMEM((ATOMS * ATOMS, HALF, LANES), jnp.float32),
             pltpu.VMEM((order, order), jnp.bfloat16),
             pltpu.VMEM((order, order), jnp.float32),
+            pltpu.VMEM(basis.shape, jnp.bfloat16),
+            pltpu.VMEM(basis.shape, jnp.bfloat16),
+            pltpu.SemaphoreType.DMA,
         ],
         compiler_params=pltpu.CompilerParams(vmem_limit_bytes=VMEM_LIMIT),
         name="grid",
@@ -427,35 +476,8 @@
 
 def block_masks(mask_ref, i, j):
     low = lax.broadcasted_iota(jnp.int32, (EDGE, LANES), 1) < EDGE
-    return jnp.where(low, mask_ref[i, j].astype(jnp.float32), mask_ref[i, j + 1].astype(jnp.float32))
-
-
-def add_kernel(scale, mask_ref, sums, core_ref, ks_ref, x0_ref):
-    rows, cols = core_ref.shape
-    across = cols // EDGE
-    for i in range(rows // EDGE):
-        for j in range(0, across, 2):
-            lanes = slice(j * EDGE, (j + 2) * EDGE)
-            high, mid, low = i * EDGE, i * EDGE + HALF, (i + 1) * EDGE
-            top, bottom = join_pair(sums[i * across + j], sums[i * across + j + 1])
-            ks_ref[high:mid, lanes] = core_ref[high:mid, lanes] + top
-            ks_ref[mid:low, lanes] = core_ref[mid:low, lanes] + bottom
-            kept = block_masks(mask_ref, i, j) * ks_ref[high:low, lanes] * scale
-            x0_ref[high:low, lanes] = kept.astype(jnp.bfloat16)
-
-
-def add_back(scale, block_mask, sums, core_ham):
-    return pl.pallas_call(
-        functools.partial(add_kernel, scale),
-        out_shape=(
-            jax.ShapeDtypeStruct(core_ham.shape, jnp.float32),
-            jax.ShapeDtypeStruct(core_ham.shape, jnp.bfloat16),
-        ),
-        in_specs=[pl.BlockSpec(memory_space=pltpu.SMEM)] + [pl.BlockSpec(memory_space=pltpu.VMEM)] * 2,
-        out_specs=(pl.BlockSpec(memory_space=pltpu.VMEM),) * 2,
-        compiler_params=pltpu.CompilerParams(vmem_limit_bytes=VMEM_LIMIT),
-        name="add_back",
-    )(block_mask, sums, core_ham)
+    left, right = mask_ref[i : i + 1, j : j + 1], mask_ref[i : i + 1, j + 1 : j + 2]
+    return jnp.where(low, left.astype(jnp.float32), right.astype(jnp.float32))
 
 
 class LineGather:
@@ -501,6 +523,10 @@
         self.send(
             jnp.logical_and(cond, fits), outer_at * self.inner + inner_from, self.a * self.inner + target, sem
         )
+
+    def begin(self):
+        self.going = self.steps()
+        next(self.going)
 
     def steps(self):
         a, b, inner = self.a, self.b, self.inner
@@ -577,68 +603,76 @@
 
 
 def run_together(*gathers):
-    going = [gather.steps() for gather in gathers]
+    going = [gather.going for gather in gathers]
     while going:
         going = [steps for steps in going if next(steps, "end") is None]
 
 
-def panel_product(left, right, acc):
-    height, width = right.shape[1], left.shape[2]
-    acc[...] = jnp.zeros_like(acc)
-    for j in range(left.shape[0]):
-        start = j * width
-        part = right[start // height, start % height : start % height + width, :]
-        acc[...] += jnp.dot(left[j], part, preferred_element_type=jnp.float32)
-
-
-def sign_kernel(scale, row_lines, col_lines, mask_ref, x0_ref, out_ref, left, right, second, mask, acc, *sems):
-    row, col = lax.axis_index("row"), lax.axis_index("col")
+def add_product(acc, left, right, place):
+    width = left.shape[2]
+    share = right.shape[1] // width
+    for part in range(share):
+        piece = right[place, part * width : (part + 1) * width, :]
+        acc[...] += jnp.dot(left[place * share + part], piece, preferred_element_type=jnp.float32)
+
+
+def first_rows(rows, outer, inner):
+    if inner == 1 or outer == 1:
+        return rows
+    share = ((outer - 1) * inner - (inner - 1)) / (2 * (outer - 1) * (inner - 1))
+    return min(rows - 16, max(16, round(share * rows / 16) * 16))
+
+
+def sign_part(plane, mask_ref, x0_ref, x3_ref, left, right, second, mask, acc, *sems):
+    row, outer, inner = plane.row, plane.outer, plane.inner
+    col = plane.a * inner + plane.b
     rows, cols = x0_ref.shape
-    along_col = LineGather(left.at.__getitem__, *col_lines, col, lambda at: (row, at), sems[0:3])
-    along_row = LineGather(right.at.__getitem__, *row_lines, row, lambda at: (at, col), sems[3:6])
-    again = LineGather(second.at.__getitem__, *row_lines, row, lambda at: (at, col), sems[6:9])
-    greet([along_col, along_row])
+    row_lines = (right.shape[0] // CORES, CORES)
+    split = first_rows(rows, outer, inner)
+
+    def turned(at):
+        return (at % outer) * inner + at // outer
+
+    gathers = [
+        LineGather(
+            lambda at: left.at[at, pl.ds(0, split)], outer, inner, col, lambda at: (row, at), sems[0:3]
+        ),
+        LineGather(right.at.__getitem__, *row_lines, row, lambda at: (at, col), sems[6:9]),
+    ]
+    if split < rows:
+        gathers.insert(
+            1,
+            LineGather(
+                lambda at: left.at[turned(at), pl.ds(split, rows - split)],
+                inner,
+                outer,
+                plane.b * outer + plane.a,
+                lambda at: (row, turned(at)),
+                sems[3:6],
+            ),
+        )
+    again = LineGather(second.at.__getitem__, *row_lines, row, lambda at: (at, col), sems[9:12])
     left[col] = x0_ref[...]
     right[row] = x0_ref[...]
-    run_together(along_col, along_row)
+    for gather in gathers:
+        gather.begin()
     for i in range(rows // EDGE):
         for j in range(0, cols // EDGE, 2):
             mask[i * EDGE : (i + 1) * EDGE, j * EDGE : (j + 2) * EDGE] = block_masks(mask_ref, i, j)
-    panel_product(left, right, acc)
+    run_together(*gathers)
+    acc[...] = jnp.zeros_like(acc)
+    for place in range(right.shape[0]):
+        add_product(acc, left, right, place)
     second[row] = (mask[...] * acc[...]).astype(jnp.bfloat16)
+    again.begin()
+    acc[...] = jnp.zeros_like(acc)
+    add_product(acc, left, second, row)
     run_together(again)
-    panel_product(left, second, acc)
-    out_ref[...] = (1.5 * x0_ref[...].astype(jnp.float32) - 0.5 * (mask[...] * acc[...])) / scale
-    for gather in (along_col, along_row, again):
+    for offset in range(1, right.shape[0]):
+        add_product(acc, left, second, lax.rem(row + offset, right.shape[0]))
+    x3_ref[...] = mask[...] * acc[...]
+    for gather in (*gathers, again):
         gather.drain()
-
-
-def sign_step(scale, block_mask, x0):
-    row_count, col_count = lax.axis_size("row"), lax.axis_size("col")
-    row_lines = (row_count // CORES, CORES)
-    outer = math.gcd(col_count, 4)
-    col_lines = (outer, col_count // outer)
-    rows, cols = x0.shape
-    return pl.pallas_call(
-        functools.partial(sign_kernel, scale, row_lines, col_lines),
-        out_shape=jax.ShapeDtypeStruct(x0.shape, jnp.float32),
-        in_specs=[pl.BlockSpec(memory_space=pltpu.SMEM), pl.BlockSpec(memory_space=pltpu.VMEM)],
-        out_specs=pl.BlockSpec(memory_space=pltpu.VMEM),
-        scratch_shapes=[
-            pltpu.VMEM((col_count, rows, cols), jnp.bfloat16),
-            pltpu.VMEM((row_count, rows, cols), jnp.bfloat16),
-            pltpu.VMEM((row_count, rows, cols), jnp.bfloat16),
-            pltpu.VMEM((rows, cols), jnp.float32),
-            pltpu.VMEM((rows, cols), jnp.float32),
-            *LineGather.semaphores(*col_lines),
-            *LineGather.semaphores(*row_lines),
-            *LineGather.semaphores(*row_lines),
-        ],
-        compiler_params=pltpu.CompilerParams(
-            vmem_limit_bytes=VMEM_LIMIT, collective_id=0, has_side_effects=True
-        ),
-        name="sign",
-    )(block_mask, x0)
 
 
 def body(density, core_ham, block_mask, send_blocks, task_atoms, basis, v_loc):
@@ -655,10 +689,11 @@
     pair = (atoms[0] * ATOMS + atoms[1]).reshape(-1)
     received, kept = send_blocks_out((outer, inner), capacity, lists, density)
     k_slot = grid_step(pair, received.reshape(-1, HALF, LANES), basis[0], v_loc)
-    sums = send_blocks_back((outer, inner), local_count, kept, k_slot.reshape(received.shape))
     scale = 1.0 / math.sqrt(16.0 * block_rows * row_count)
-    ks_matrix, x0 = add_back(scale, block_mask, sums, core_ham)
-    return (ks_matrix, sign_step(scale, block_mask, x0))
+    ham_tile, x0, x3 = send_blocks_back(
+        scale, (outer, inner), kept, k_slot.reshape(received.shape), block_mask, core_ham
+    )
+    return (core_ham + ham_tile, (1.5 * x0.astype(jnp.float32) - 0.5 * x3) / scale)
 
 
 def solution(mesh):

time: 138 us -> 135 us (0.978)
  Pallas kernels: 131 us -> 126 us
  other arithmetic: 0.72 us -> 4.61 us
  local copies, waits for them, and re-layouts: 4.81 us -> 2.95 us
    pallas_call x3 -> x1, Pallas kernels: 76.8 us -> 71.9 us  [send_blocks_back(): pl.pallas_call(functools.partial(back_kernel, scale, outer, inner, row_co...]
    div x0 -> x1, other arithmetic: none -> 1.99 us  [body(): (1.5 * x0.astype(jnp.float32) - 0.5 * x3) / scale]
    add x0 -> x1, other arithmetic: none -> 1.9 us  [body(): core_ham + ham_tile]
    unnamed x5 -> x6, local copies, waits for them, and re-layouts: 3.31 us -> 1.45 us
where the time goes in v3:
time: 135 us; the launch traced here: 134 us
  Pallas kernels  126 us (93%)
  other arithmetic  4.61 us (3%)
  local copies, waits for them, and re-layouts  2.95 us (2%)
    pallas_call x1, Pallas kernels, send_blocks_back(): pl.pallas_call(functools.partial(back_kernel, scale, outer, inner, row_co...  71.9 us
    pallas_call x1, Pallas kernels, send_blocks_out(): pl.pallas_call(functools.partial(send_kernel, outer, inner, row_count), o...  34.5 us
    pallas_call x1, Pallas kernels, grid_step(): pl.pallas_call(functools.partial(grid_kernel, chunk), out_shape=jax.Shape...  19.7 us

profile of v3, /device:TPU:1, one launch (start us, length us, event | category | flops | bytes accessed | tf_op | source)
XLA Modules:
  0.0 134.3 jit_solution(7854116712301628448)
XLA Ops:
  0.6 0.8 copy.10
  1.4 0.1 reshape_squeeze.3
  1.5 0.1 reshape.23
  1.6 0.6 pad.4.index_ref.lists_ref
  2.2 34.5 %send_out.1 = (bf16[32,8,32,128]{3,2,1,0:T(8,128)(2,1)}, s32[8,128]{1,0:T(8,128)}) custom-call(s32[8,128]{1,0:T(8,128)} %pad.4.index_ref.lists_ref, s32[8,128]{1,0:T(8,128)} %pad.4.index_ref.lists_ref, bf16[512,256]{1,0:T(8,128)(2,1)} %density_ref.1), custom_call_target="tpu_custom_call" | custom-call | tf_op jit(solution)/shard_map/send_out/pallas_call | solution.py:184
  36.7 0.7 slice_add_fusion
  37.4 0.1 copy.12
  37.5 0.7 add.13.pair_ref
  38.1 0.0 copy-start.1
  38.1 19.7 %grid.1 = bf16[256,32,128]{2,1,0:T(8,128)(2,1)} custom-call(s32[256]{0:T(256)} %add.13.pair_ref, bf16[256,32,128]{2,1,0:T(8,128)(2,1)} %bitcast.9, bf16[1024,2048]{1,0:T(8,128)(2,1)} %bitcast.8, f32[1,2048]{1,0:T(1,128)} %vloc_ref.1), custom_call_target="tpu_custom_call" | custom-call | tf_op jit(solution)/shard_map/grid/pallas_call | solution.py:454
  57.8 0.0 copy-start
  57.8 0.0 copy-done.1
  57.8 0.7 copy.13.mask_ref
  58.5 71.9 %back_and_sign.1 = (f32[512,256]{1,0:T(8,128)}, bf16[512,256]{1,0:T(8,128)(2,1)}, f32[512,256]{1,0:T(8,128)}) custom-call(s32[8,128]{1,0:T(8,128)} %get-tuple-element.7.kept_ref, s32[8,4]{1,0:T(8,128)} %copy.13.mask_ref, bf16[32,8,32,128]{3,2,1,0:T(8,128)(2,1)} %bitcast.7, f32[512,256]{1,0:T(8,128)} %core_ref.1), custom_call_target="tpu_custom_call" | custom-call | tf_op jit(solution)/shard_map/back_and_sign/pallas_call | solution.py:348
  130.4 2.0 %subtract_multiply_fusion = f32[512,256]{1,0:T(8,128)} fusion(f32[512,256]{1,0:T(8,128)} %get-tuple-element.11, bf16[512,256]{1,0:T(8,128)(2,1)} %get-tuple-element.10), kind=kLoop, calls=%fused_computation | loop fusion | flops 655360 | bytes 1310720 | tf_op jit(solution)/shard_map/div | solution.py:696
  132.4 0.0 copy-done
  132.4 1.9 %add.14 = f32[512,256]{1,0:T(8,128)} add(f32[512,256]{1,0:T(8,128)S(1)} %copy-done, f32[512,256]{1,0:T(8,128)} %get-tuple-element.9) | non-fusion elementwise | flops 131072 | bytes 1572864 | tf_op jit(solution)/shard_map/add | solution.py:696
  (2 shorter events, 0.0 us)
Async XLA Ops:
  38.1 19.7 %copy-start.1 = (s32[8,4]{0,1:T(4,128)S(1)}, s32[8,4]{0,1:T(4,128)}, u32[]{:S(2)}) copy-start(s32[8,4]{0,1:T(4,128)} %param.9) | copy-start | bytes 388
  57.8 74.6 %copy-start = (f32[512,256]{1,0:T(8,128)S(1)}, f32[512,256]{1,0:T(8,128)}, u32[]{:S(2)}) copy-start(f32[512,256]{1,0:T(8,128)} %core_ref.1) | copy-start | bytes 1572868

commit v4 on v3

--- a/solution.py
+++ b/solution.py
@@ -77,7 +77,8 @@
     for tile in (own, *arrived[0], *arrived[1]):
         tile[count] = jnp.zeros((HALF, LANES), tile.dtype)
     plane.greet(entries)
-    lists[a] = lists_ref[...]
+    lists[a] = jnp.zeros(lists.shape[1:], jnp.int32)
+    lists[a, 0 : lists_ref.shape[0], 0 : lists_ref.shape[1]] = lists_ref[...]
     for i in range(rows // EDGE):
         for j in range(0, across, 2):
             lanes = slice(j * EDGE, (j + 2) * EDGE)
@@ -106,8 +107,12 @@
 
     def serve(tile, source, number):
         def pick(offset, place):
+            target = plane.owner(place, a)
             for slot in range(slots):
-                stage[source, offset, slot] = tile[number(place * slots + slot)]
+                found = number(slot, target)
+                local = jnp.where(found >= 0, found, count)
+                stage[source, offset, slot] = tile[local]
+                kept_ref[source, place * slots + slot] = local
 
         def one(offset, carry):
             place = plane.peer(offset)
@@ -147,7 +152,7 @@
                     pass_on(d, way, step).start()
 
         if d == 0:
-            serve(own, a, lambda at: index_ref[a, at])
+            serve(own, a, lambda slot, at: index_ref[slot, at])
             continue
         for way, step in enumerate((1, -1)):
             source = a - d * step
@@ -157,11 +162,8 @@
                 copy = pltpu.make_async_copy(lists.at[source], lists_smem.at[source], list_sem)
                 copy.start()
                 copy.wait()
-                serve(arrived[way][d - 1], source, lambda at: lists_smem[source, a, at])
-
-    kept_ref[...] = jnp.zeros_like(kept_ref)
-    for i in range(outer):
-        kept_ref[i : i + 1, :] = lists[i, pl.ds(a, 1), :]
+                serve(arrived[way][d - 1], source, lambda slot, at: lists_smem[source, slot, at])
+
     for d in range(outer - 1):
         for way, step in enumerate((1, -1)):
 
@@ -175,8 +177,13 @@
     pltpu.make_async_copy(out_ref, out_ref, recv_sem).wait()
 
 
-def send_blocks_out(lines, slots, lists, density):
+def up_to(size, step):
+    return size + -size % step
+
+
+def send_blocks_out(lines, lists, density):
     outer, inner = lines
+    slots, devices = lists.shape
     row_count, col_count = lax.axis_size("row"), lax.axis_size("col")
     plane_count = row_count * inner
     count = (density.shape[0] // EDGE) * (density.shape[1] // EDGE)
@@ -185,14 +192,14 @@
         functools.partial(send_kernel, outer, inner, row_count),
         out_shape=(
             jax.ShapeDtypeStruct((row_count * col_count, slots, HALF, LANES), jnp.bfloat16),
-            jax.ShapeDtypeStruct(lists.shape, jnp.int32),
+            jax.ShapeDtypeStruct((up_to(outer, 8), up_to(plane_count * slots, LANES)), jnp.int32),
         ),
         in_specs=[pl.BlockSpec(memory_space=pltpu.SMEM), vmem, vmem],
-        out_specs=(pl.BlockSpec(memory_space=pl.ANY), vmem),
+        out_specs=(pl.BlockSpec(memory_space=pl.ANY), pl.BlockSpec(memory_space=pltpu.SMEM)),
         scratch_shapes=[
             pltpu.VMEM((count + 1, HALF, LANES), jnp.bfloat16),
-            pltpu.VMEM((outer, *lists.shape), jnp.int32),
-            pltpu.SMEM((outer, *lists.shape), jnp.int32),
+            pltpu.VMEM((outer, up_to(slots, 8), up_to(devices, LANES)), jnp.int32),
+            pltpu.SMEM((outer, up_to(slots, 8), up_to(devices, LANES)), jnp.int32),
             pltpu.VMEM((outer, plane_count, slots, HALF, LANES), jnp.bfloat16),
             pltpu.SemaphoreType.DMA,
             pltpu.SemaphoreType.DMA,
@@ -382,19 +389,25 @@
 
 
 def grid_kernel(
-    chunk, pair_ref, recv_ref, basis_hbm, vloc_ref, out_ref, sums, pair_mat, k_all, basis_ref, weighted, sem
+    chunk, atoms_ref, recv_ref, basis_hbm, vloc_ref, out_ref, sums, pair_mat, k_all, basis_ref, weighted, sem
 ):
     cells = basis_ref.shape[1]
     load = pltpu.make_async_copy(basis_hbm, basis_ref, sem)
     load.start()
     sums[...] = jnp.zeros_like(sums)
 
-    def add_slot(slot, carry):
-        at = pair_ref[slot]
-        sums[at] = sums[at] + recv_ref[slot].astype(jnp.float32)
+    owners, slots = recv_ref.shape[:2]
+
+    def pair(owner, slot):
+        return atoms_ref[0, slot, owner] * ATOMS + atoms_ref[1, slot, owner]
+
+    def add_slots(owner, carry):
+        for slot in range(slots):
+            at = pair(owner, slot)
+            sums[at] = sums[at] + recv_ref[owner, slot].astype(jnp.float32)
         return carry
 
-    lax.fori_loop(0, recv_ref.shape[0], add_slot, 0, unroll=8)
+    lax.fori_loop(0, owners, add_slots, 0)
 
     def assemble(a, carry):
         row = pl.multiple_of(a * EDGE, EDGE)
@@ -406,29 +419,34 @@
         return carry
 
     lax.fori_loop(0, ATOMS, assemble, 0)
+    columns = 4 * EDGE
+    tiles = [slice(start, start + columns) for start in range(0, ATOMS * EDGE, columns)]
+    for m, high in enumerate(tiles):
+        for low in tiles[m + 1 :]:
+            turned = pair_mat[low, high].astype(jnp.float32).T
+            pair_mat[high, low] = (pair_mat[high, low].astype(jnp.float32) + turned).astype(jnp.bfloat16)
     load.wait()
 
     def integrate(step, carry):
         at = pl.ds(pl.multiple_of(step * chunk, chunk), chunk)
-        vals = basis_ref[:, at]
-        mixed = jnp.dot(pair_mat[...], vals, preferred_element_type=jnp.float32)
-        wide = vals.astype(jnp.float32)
-        rho = jnp.sum(wide * mixed, axis=0, keepdims=True)
+        rho = jnp.zeros((1, chunk), jnp.float32)
+        for high in tiles:
+            mixed = jnp.dot(
+                pair_mat[high, high.start :], basis_ref[high.start :, at], preferred_element_type=jnp.float32
+            )
+            rho += jnp.sum(basis_ref[high, at].astype(jnp.float32) * mixed, axis=0, keepdims=True)
+        wide = basis_ref[:, at].astype(jnp.float32)
         pot = vloc_ref[:, at] + 0.5 * rho / jnp.sqrt(1.0 + rho * rho)
         weighted[:, at] = (wide * pot).astype(jnp.bfloat16)
         return carry
 
     lax.fori_loop(0, cells // chunk, integrate, 0)
-    columns = 4 * EDGE
-
-    def multiply(step, carry):
-        at = pl.ds(pl.multiple_of(step * columns, columns), columns)
-        k_all[:, at] = lax.dot_general(
-            weighted[...], basis_ref[at, :], (((1,), (1,)), ((), ())), preferred_element_type=jnp.float32
+    for n, low in enumerate(tiles):
+        k_all[: low.stop, low] = lax.dot_general(
+            weighted[: low.stop, :], basis_ref[low, :], (((1,), (1,)), ((), ())), preferred_element_type=jnp.float32
         )
-        return carry
-
-    lax.fori_loop(0, k_all.shape[1] // columns, multiply, 0)
+        for high in tiles[:n]:
+            k_all[low, high] = k_all[high, low].T
 
     def split(a, carry):
         row = pl.multiple_of(a * EDGE, EDGE)
@@ -441,14 +459,15 @@
 
     lax.fori_loop(0, ATOMS, split, 0)
 
-    def give_slot(slot, carry):
-        out_ref[slot] = sums[pair_ref[slot]].astype(jnp.bfloat16)
+    def give_slots(owner, carry):
+        for slot in range(slots):
+            out_ref[owner, slot] = sums[pair(owner, slot)].astype(jnp.bfloat16)
         return carry
 
-    lax.fori_loop(0, out_ref.shape[0], give_slot, 0, unroll=8)
-
-
-def grid_step(pair, received, basis, v_loc):
+    lax.fori_loop(0, owners, give_slots, 0)
+
+
+def grid_step(atoms, received, basis, v_loc):
     order = ATOMS * EDGE
     chunk = math.gcd(basis.shape[1], 512)
     return pl.pallas_call(
@@ -471,12 +490,12 @@
         ],
         compiler_params=pltpu.CompilerParams(vmem_limit_bytes=VMEM_LIMIT),
         name="grid",
-    )(pair, received, basis, v_loc)
+    )(atoms, received, basis, v_loc)
 
 
 def block_masks(mask_ref, i, j):
     low = lax.broadcasted_iota(jnp.int32, (EDGE, LANES), 1) < EDGE
-    left, right = mask_ref[i : i + 1, j : j + 1], mask_ref[i : i + 1, j + 1 : j + 2]
+    left, right = mask_ref[j : j + 1, i : i + 1], mask_ref[j + 1 : j + 2, i : i + 1]
     return jnp.where(low, left.astype(jnp.float32), right.astype(jnp.float32))
 
 
@@ -675,25 +694,35 @@
         gather.drain()
 
 
+def finish_kernel(scale, core_ref, ham_ref, x0_ref, x3_ref, ks_ref, sign_ref):
+    ks_ref[...] = core_ref[...] + ham_ref[...]
+    sign_ref[...] = (1.5 * x0_ref[...].astype(jnp.float32) - 0.5 * x3_ref[...]) / scale
+
+
+def finish(scale, core_ham, ham_tile, x0, x3):
+    rows, cols = core_ham.shape
+    share = pl.BlockSpec((rows // 2, cols), lambda i: (i, 0))
+    return pl.pallas_call(
+        functools.partial(finish_kernel, scale),
+        out_shape=(jax.ShapeDtypeStruct(core_ham.shape, jnp.float32),) * 2,
+        grid=(2,),
+        in_specs=[share] * 4,
+        out_specs=(share,) * 2,
+        compiler_params=pltpu.CompilerParams(vmem_limit_bytes=VMEM_LIMIT),
+        name="finish",
+    )(core_ham, ham_tile, x0, x3)
+
+
 def body(density, core_ham, block_mask, send_blocks, task_atoms, basis, v_loc):
     row_count, col_count = lax.axis_size("row"), lax.axis_size("col")
     block_rows = density.shape[0] // EDGE
-    local_count = block_rows * (density.shape[1] // EDGE)
-    capacity = send_blocks.shape[2]
     outer = math.gcd(col_count, 4)
     inner = col_count // outer
-    slots = send_blocks[0].reshape(row_count, outer, inner * capacity)
-    lists = jnp.where(slots >= 0, slots, local_count).transpose(1, 0, 2).reshape(outer, -1)
-    lists = jnp.pad(lists, ((0, -outer % 8), (0, -lists.shape[1] % 128)))
-    atoms = task_atoms[:, 0]
-    pair = (atoms[0] * ATOMS + atoms[1]).reshape(-1)
-    received, kept = send_blocks_out((outer, inner), capacity, lists, density)
-    k_slot = grid_step(pair, received.reshape(-1, HALF, LANES), basis[0], v_loc)
+    received, kept = send_blocks_out((outer, inner), send_blocks[0].T, density)
+    k_slot = grid_step(task_atoms[:, 0].transpose(0, 2, 1), received, basis[0], v_loc)
     scale = 1.0 / math.sqrt(16.0 * block_rows * row_count)
-    ham_tile, x0, x3 = send_blocks_back(
-        scale, (outer, inner), kept, k_slot.reshape(received.shape), block_mask, core_ham
-    )
-    return (core_ham + ham_tile, (1.5 * x0.astype(jnp.float32) - 0.5 * x3) / scale)
+    parts = send_blocks_back(scale, (outer, inner), kept, k_slot, block_mask.T, core_ham)
+    return finish(scale, core_ham, *parts)
 
 
 def solution(mesh):

time: 135 us -> 127 us (0.941)
  other arithmetic: 4.61 us -> 0 us
  local copies, waits for them, and re-layouts: 2.95 us -> 0 us
    pallas_call x1, Pallas kernels: 19.7 us -> 16.9 us  [grid_step(): pl.pallas_call(functools.partial(grid_kernel, chunk), out_shape=jax.Shape...]
    add x2 -> x0, other arithmetic: 2.61 us -> none  [the longest x1 1.9 us: body(): core_ham + ham_tile]
    pallas_call x0 -> x1, Pallas kernels: none -> 2.29 us  [finish(): pl.pallas_call(functools.partial(finish_kernel, scale), out_shape=(jax.Sh...]
    div x1 -> x0, other arithmetic: 1.99 us -> none  [body(): (1.5 * x0.astype(jnp.float32) - 0.5 * x3) / scale]
    unnamed x6 -> x0, local copies, waits for them, and re-layouts: 1.45 us -> none
where the time goes in v4:
time: 127 us; the launch traced here: 126 us
  Pallas kernels  126 us (99%)
    pallas_call x1, Pallas kernels, send_blocks_back(): pl.pallas_call(functools.partial(back_kernel, scale, outer, inner, row_co...  71.8 us
    pallas_call x1, Pallas kernels, send_blocks_out(): pl.pallas_call(functools.partial(send_kernel, outer, inner, row_count), o...  34.6 us
    pallas_call x1, Pallas kernels, grid_step(): pl.pallas_call(functools.partial(grid_kernel, chunk), out_shape=jax.Shape...  16.9 us

profile of v4, /device:TPU:1, one launch (start us, length us, event | category | flops | bytes accessed | tf_op | source)
XLA Modules:
  0.0 126.3 jit_solution(6876853150568556045)
XLA Ops:
  0.6 34.6 %send_out.1 = (bf16[32,8,32,128]{3,2,1,0:T(8,128)(2,1)}, s32[8,128]{1,0:T(8,128)}) custom-call(s32[8,32]{1,0:T(8,128)} %bitcast.9, s32[8,32]{1,0:T(8,128)} %bitcast.10, bf16[512,256]{1,0:T(8,128)(2,1)} %density_ref.1), custom_call_target="tpu_custom_call" | custom-call | tf_op jit(solution)/shard_map/send_out/pallas_call | solution.py:191
  35.3 16.9 %grid.1.slots_ref = bf16[32,8,32,128]{3,2,1,0:T(8,128)(2,1)} custom-call(s32[2,8,32]{2,1,0:T(8,128)} %bitcast.11, bf16[32,8,32,128]{3,2,1,0:T(8,128)(2,1)} %get-tuple-element.8.recv_ref, bf16[1024,2048]{1,0:T(8,128)(2,1)} %bitcast.8, f32[1,2048]{1,0:T(1,128)} %vloc_ref.1), custom_call_target="tpu_custom_call" | custom-call | tf_op jit(solution)/shard_map/grid/pallas_call | solution.py:473
  52.2 71.8 %back_and_sign.1 = (f32[512,256]{1,0:T(8,128)}, bf16[512,256]{1,0:T(8,128)(2,1)}, f32[512,256]{1,0:T(8,128)}) custom-call(s32[8,128]{1,0:T(8,128)} %get-tuple-element.7.kept_ref, s32[4,8]{1,0:T(4,128)} %bitcast.12, bf16[32,8,32,128]{3,2,1,0:T(8,128)(2,1)} %grid.1.slots_ref, f32[512,256]{1,0:T(8,128)} %core_ref.3), custom_call_target="tpu_custom_call" | custom-call | tf_op jit(solution)/shard_map/back_and_sign/pallas_call | solution.py:355
  124.0 2.3 %finish.1 = (f32[512,256]{1,0:T(8,128)}, f32[512,256]{1,0:T(8,128)}) custom-call(f32[512,256]{1,0:T(8,128)} %core_ref.3, f32[512,256]{1,0:T(8,128)} %get-tuple-element.9.ham_ref, bf16[512,256]{1,0:T(8,128)(2,1)} %get-tuple-element.10.x0_ref, f32[512,256]{1,0:T(8,128)} %get-tuple-element.11.x3_ref), custom_call_target="tpu_custom_call" | custom-call | tf_op jit(solution)/shard_map/finish/pallas_call | solution.py:705

commit v5 on v4

--- a/solution.py
+++ b/solution.py
@@ -13,6 +13,7 @@
 HALF = EDGE // 2
 LANES = 2 * EDGE
 CORES = 2
+CHUNKS = 4
 MESH = pl.DeviceIdType.MESH
 VMEM_LIMIT = 56 * 1024 * 1024
 
@@ -76,7 +77,6 @@
     arrived = (rest[3 : 2 + outer], rest[2 + outer :])
     for tile in (own, *arrived[0], *arrived[1]):
         tile[count] = jnp.zeros((HALF, LANES), tile.dtype)
-    plane.greet(entries)
     lists[a] = jnp.zeros(lists.shape[1:], jnp.int32)
     lists[a, 0 : lists_ref.shape[0], 0 : lists_ref.shape[1]] = lists_ref[...]
     for i in range(rows // EDGE):
@@ -87,6 +87,7 @@
             first, second = split_pair(top, bottom)
             own[i * across + j] = first.astype(own.dtype)
             own[i * across + j + 1] = second.astype(own.dtype)
+    plane.greet(entries)
 
     def passes(d, step):
         source, target = a - d * step, a + step
@@ -135,12 +136,16 @@
 
     entry_steps = entries.steps()
     for d in range(outer):
-        next(entry_steps)
+        next(entry_steps, None)
         if d:
             for way, step in enumerate((1, -1)):
-
-                @pl.when(jnp.logical_and(a - d * step >= 0, a - d * step < outer))
+                source = a - d * step
+
+                @pl.when(jnp.logical_and(source >= 0, source < outer))
                 def _():
+                    copy = pltpu.make_async_copy(lists.at[source], lists_smem.at[source], list_sem)
+                    copy.start()
+                    copy.wait()
                     tile = arrived[way][d - 1].at[pl.ds(0, count)]
                     pltpu.make_async_copy(tile, tile, tile_recv.at[way, d - 1]).wait()
 
@@ -159,9 +164,6 @@
 
             @pl.when(jnp.logical_and(source >= 0, source < outer))
             def _():
-                copy = pltpu.make_async_copy(lists.at[source], lists_smem.at[source], list_sem)
-                copy.start()
-                copy.wait()
                 serve(arrived[way][d - 1], source, lambda slot, at: lists_smem[source, slot, at])
 
     for d in range(outer - 1):
@@ -218,7 +220,7 @@
 
 def back_kernel(
     scale, outer, inner, row_count, kept_ref, mask_ref, slots_ref, core_ref, ham_ref, x0_ref, x3_ref,
-    landed, wide, total, sums, arriving, land_sem, send_sem, line_send, line_recv, *rest
+    landed, wide, first_total, second_total, sums, arriving, land_sem, send_sem, line_send, line_recv, *rest
 ):
     plane = Plane(outer, inner, row_count)
     a, b = plane.a, plane.b
@@ -248,7 +250,7 @@
             slots_ref.at[plane.owner(plane.place, target)], landed.at[target, plane.place], land_sem.at[target]
         ).start()
 
-    def combine(target):
+    def combine(target, total):
         pltpu.make_async_copy(landed.at[target], landed.at[target], land_sem.at[target]).wait()
         wide[...] = landed[target].astype(jnp.float32).reshape(wide.shape)
         numbers = lax.broadcasted_iota(jnp.int32, (count, terms), 0)
@@ -298,26 +300,35 @@
         pltpu.make_async_copy(sent, sent, send_sem.at[target]).wait()
 
     nth(0, send_plane)
+    totals = (first_total, second_total)
+
+    def pass_total(k, with_line):
+        total = totals[k % 2]
+
+        def handle(target):
+            for side, step in ((0, 1), (1, -1)):
+                inside = jnp.logical_and(a - step >= 0, a - step < outer)
+                fits = inside if with_line else jnp.logical_not(inside)
+
+                @pl.when(jnp.logical_and((target - a) * step > 0, fits))
+                def _():
+                    if with_line:
+                        wait_line(target, side)
+                        total[...] += arriving[target, side].astype(jnp.float32).reshape(total.shape)
+                    sums[target] = total[...].astype(jnp.bfloat16).reshape(sums.shape[1:])
+                    pass_on(target, step, side).start()
+
+        nth(k, handle)
+
     for k in range(outer):
         nth(k, sent_plane)
         if k + 1 < outer:
             nth(k + 1, send_plane)
-
-        def handle(target):
-            combine(target)
-            for side, step in ((0, 1), (1, -1)):
-
-                @pl.when((target - a) * step > 0)
-                def _():
-                    @pl.when(jnp.logical_and(a - step >= 0, a - step < outer))
-                    def _():
-                        wait_line(target, side)
-                        total[...] += arriving[target, side].astype(jnp.float32).reshape(total.shape)
-
-                    sums[target] = total[...].astype(jnp.bfloat16).reshape(sums.shape[1:])
-                    pass_on(target, step, side).start()
-
-        nth(k, handle)
+        nth(k, lambda target: combine(target, totals[k % 2]))
+        pass_total(k, False)
+        if k:
+            pass_total(k - 1, True)
+    total = totals[(outer - 1) % 2]
     for side, step in ((0, 1), (1, -1)):
 
         @pl.when(jnp.logical_and(a - step >= 0, a - step < outer))
@@ -365,6 +376,7 @@
             pltpu.VMEM((outer, plane_count, slots, HALF, LANES), jnp.bfloat16),
             pltpu.VMEM((plane_count * slots * HALF, LANES), jnp.float32),
             pltpu.VMEM((count * HALF, LANES), jnp.float32),
+            pltpu.VMEM((count * HALF, LANES), jnp.float32),
             pltpu.VMEM((outer, count, HALF, LANES), jnp.bfloat16),
             pltpu.VMEM((outer, 2, count, HALF, LANES), jnp.bfloat16),
             pltpu.SemaphoreType.DMA((outer,)),
@@ -376,10 +388,13 @@
             pltpu.VMEM((row_count, rows, cols), jnp.bfloat16),
             pltpu.VMEM((rows, cols), jnp.float32),
             pltpu.VMEM((rows, cols), jnp.float32),
-            *LineGather.semaphores(outer, inner),
-            *LineGather.semaphores(inner, outer),
             *LineGather.semaphores(*row_lines),
-            *LineGather.semaphores(*row_lines),
+            *[
+                sem
+                for turned in turned_chunks(outer, inner)
+                for sem in LineGather.semaphores(*((inner, outer) if turned else (outer, inner)))
+            ],
+            *LineGather.semaphores(*row_lines) * CHUNKS,
         ],
         compiler_params=pltpu.CompilerParams(
             vmem_limit_bytes=VMEM_LIMIT, collective_id=2, has_side_effects=True
@@ -545,7 +560,7 @@
 
     def begin(self):
         self.going = self.steps()
-        next(self.going)
+        next(self.going, None)
 
     def steps(self):
         a, b, inner = self.a, self.b, self.inner
@@ -570,7 +585,8 @@
                 if d > 0 or way == 0:
                     for side, hop in enumerate((1, -1)):
                         self.along_inner(have, source, b, hop, self.in_sem.at[d * 2 + way, side])
-            yield
+            if inner > 1 or d < self.outer - 1:
+                yield
         used = 2 * self.outer
         for e in range(1, inner):
             for outer_at in range(self.outer):
@@ -587,7 +603,8 @@
                         self.along_inner(have, outer_at, origin, step, self.in_sem.at[used, way])
                 if e < inner - 1:
                     used += 1
-            yield
+            if e < inner - 1:
+                yield
 
     def drain(self):
         for cond, describe in self.sent:
@@ -621,25 +638,20 @@
     pl.semaphore_wait(barrier, count)
 
 
-def run_together(*gathers):
-    going = [gather.going for gather in gathers]
-    while going:
-        going = [steps for steps in going if next(steps, "end") is None]
-
-
-def add_product(acc, left, right, place):
+def add_product(acc, left, right, place, rows=slice(None)):
     width = left.shape[2]
     share = right.shape[1] // width
     for part in range(share):
         piece = right[place, part * width : (part + 1) * width, :]
-        acc[...] += jnp.dot(left[place * share + part], piece, preferred_element_type=jnp.float32)
-
-
-def first_rows(rows, outer, inner):
+        acc[rows, :] += jnp.dot(left[place * share + part, rows, :], piece, preferred_element_type=jnp.float32)
+
+
+def turned_chunks(outer, inner):
     if inner == 1 or outer == 1:
-        return rows
+        return (False,) * CHUNKS
     share = ((outer - 1) * inner - (inner - 1)) / (2 * (outer - 1) * (inner - 1))
-    return min(rows - 16, max(16, round(share * rows / 16) * 16))
+    straight = min(CHUNKS, max(0, round(share * CHUNKS)))
+    return (False,) * straight + (True,) * (CHUNKS - straight)
 
 
 def sign_part(plane, mask_ref, x0_ref, x3_ref, left, right, second, mask, acc, *sems):
@@ -647,50 +659,65 @@
     col = plane.a * inner + plane.b
     rows, cols = x0_ref.shape
     row_lines = (right.shape[0] // CORES, CORES)
-    split = first_rows(rows, outer, inner)
+    height = rows // CHUNKS
 
     def turned(at):
         return (at % outer) * inner + at // outer
 
-    gathers = [
-        LineGather(
-            lambda at: left.at[at, pl.ds(0, split)], outer, inner, col, lambda at: (row, at), sems[0:3]
-        ),
-        LineGather(right.at.__getitem__, *row_lines, row, lambda at: (at, col), sems[6:9]),
-    ]
-    if split < rows:
-        gathers.insert(
-            1,
-            LineGather(
-                lambda at: left.at[turned(at), pl.ds(split, rows - split)],
+    def chunk_gather(number, is_turned):
+        share = pl.ds(number * height, height)
+        own_sems = sems[3 + 3 * number : 6 + 3 * number]
+        if is_turned:
+            return LineGather(
+                lambda at: left.at[turned(at), share],
                 inner,
                 outer,
                 plane.b * outer + plane.a,
                 lambda at: (row, turned(at)),
-                sems[3:6],
-            ),
-        )
-    again = LineGather(second.at.__getitem__, *row_lines, row, lambda at: (at, col), sems[9:12])
+                own_sems,
+            )
+        return LineGather(lambda at: left.at[at, share], outer, inner, col, lambda at: (row, at), own_sems)
+
+    def again_gather(number):
+        share = pl.ds(number * height, height)
+        own_sems = sems[3 * (1 + CHUNKS + number) : 3 * (2 + CHUNKS + number)]
+        return LineGather(lambda at: second.at[at, share], *row_lines, row, lambda at: (at, col), own_sems)
+
+    across_rows = LineGather(right.at.__getitem__, *row_lines, row, lambda at: (at, col), sems[0:3])
+    chunks = [chunk_gather(number, is_turned) for number, is_turned in enumerate(turned_chunks(outer, inner))]
+    again = [again_gather(number) for number in range(CHUNKS)]
     left[col] = x0_ref[...]
     right[row] = x0_ref[...]
-    for gather in gathers:
-        gather.begin()
+    chunks[0].begin()
+    across_rows.begin()
     for i in range(rows // EDGE):
         for j in range(0, cols // EDGE, 2):
             mask[i * EDGE : (i + 1) * EDGE, j * EDGE : (j + 2) * EDGE] = block_masks(mask_ref, i, j)
-    run_together(*gathers)
+    acc[...] = jnp.zeros_like(acc)
+    going, waiting = [across_rows, chunks[0]], chunks[1:]
+    while going:
+        if waiting:
+            waiting[0].begin()
+        begun = waiting[:1]
+        waiting = waiting[1:]
+        for gather in list(going):
+            if next(gather.going, "end") is None:
+                continue
+            going.remove(gather)
+            if gather in chunks:
+                number = chunks.index(gather)
+                share = slice(number * height, (number + 1) * height)
+                for place in range(right.shape[0]):
+                    add_product(acc, left, right, place, share)
+                second[row, share, :] = (mask[share, :] * acc[share, :]).astype(jnp.bfloat16)
+                again[number].begin()
+                begun.append(again[number])
+        going += begun
     acc[...] = jnp.zeros_like(acc)
     for place in range(right.shape[0]):
-        add_product(acc, left, right, place)
-    second[row] = (mask[...] * acc[...]).astype(jnp.bfloat16)
-    again.begin()
-    acc[...] = jnp.zeros_like(acc)
-    add_product(acc, left, second, row)
-    run_together(again)
-    for offset in range(1, right.shape[0]):
-        add_product(acc, left, second, lax.rem(row + offset, right.shape[0]))
+        add_product(acc, left, second, place)
     x3_ref[...] = mask[...] * acc[...]
-    for gather in (*gathers, again):
+    for gather in (across_rows, *chunks, *again):
         gather.drain()
 
 

time: 127 us -> 130 us (1.024)
  Pallas kernels: 126 us -> 129 us
    pallas_call x1, Pallas kernels: 71.8 us -> 76 us  [send_blocks_back(): pl.pallas_call(functools.partial(back_kernel, scale, outer, inner, row_co...]
where the time goes in v5:
time: 130 us
  Pallas kernels  129 us (99%)
    pallas_call x1, Pallas kernels, send_blocks_back(): pl.pallas_call(functools.partial(back_kernel, scale, outer, inner, row_co...  76 us
    pallas_call x1, Pallas kernels, send_blocks_out(): pl.pallas_call(functools.partial(send_kernel, outer, inner, row_count), o...  33.9 us
    pallas_call x1, Pallas kernels, grid_step(): pl.pallas_call(functools.partial(grid_kernel, chunk), out_shape=jax.Shape...  16.9 us

profile of v5, /device:TPU:1, one launch (start us, length us, event | category | flops | bytes accessed | tf_op | source)
XLA Modules:
  0.0 129.8 jit_solution(13475661816890545751)
XLA Ops:
  0.6 33.9 %send_out.1 = (bf16[32,8,32,128]{3,2,1,0:T(8,128)(2,1)}, s32[8,128]{1,0:T(8,128)}) custom-call(s32[8,32]{1,0:T(8,128)} %bitcast.9, s32[8,32]{1,0:T(8,128)} %bitcast.10, bf16[512,256]{1,0:T(8,128)(2,1)} %density_ref.1), custom_call_target="tpu_custom_call" | custom-call | tf_op jit(solution)/shard_map/send_out/pallas_call | solution.py:193
  34.5 16.9 %grid.1.slots_ref = bf16[32,8,32,128]{3,2,1,0:T(8,128)(2,1)} custom-call(s32[2,8,32]{2,1,0:T(8,128)} %bitcast.11, bf16[32,8,32,128]{3,2,1,0:T(8,128)(2,1)} %get-tuple-element.8.recv_ref, bf16[1024,2048]{1,0:T(8,128)(2,1)} %bitcast.8, f32[1,2048]{1,0:T(1,128)} %vloc_ref.1), custom_call_target="tpu_custom_call" | custom-call | tf_op jit(solution)/shard_map/grid/pallas_call | solution.py:488
  51.4 76.0 %back_and_sign.1 = (f32[512,256]{1,0:T(8,128)}, bf16[512,256]{1,0:T(8,128)(2,1)}, f32[512,256]{1,0:T(8,128)}) custom-call(s32[8,128]{1,0:T(8,128)} %get-tuple-element.7.kept_ref, s32[4,8]{1,0:T(4,128)} %bitcast.12, bf16[32,8,32,128]{3,2,1,0:T(8,128)(2,1)} %grid.1.slots_ref, f32[512,256]{1,0:T(8,128)} %core_ref.3), custom_call_target="tpu_custom_call" | custom-call | tf_op jit(solution)/shard_map/back_and_sign/pallas_call | solution.py:366
  127.5 2.3 %finish.1 = (f32[512,256]{1,0:T(8,128)}, f32[512,256]{1,0:T(8,128)}) custom-call(f32[512,256]{1,0:T(8,128)} %core_ref.3, f32[512,256]{1,0:T(8,128)} %get-tuple-element.9.ham_ref, bf16[512,256]{1,0:T(8,128)(2,1)} %get-tuple-element.10.x0_ref, f32[512,256]{1,0:T(8,128)} %get-tuple-element.11.x3_ref), custom_call_target="tpu_custom_call" | custom-call | tf_op jit(solution)/shard_map/finish/pallas_call | solution.py:732

commit v6 on v5

--- a/solution.py
+++ b/solution.py
@@ -688,18 +688,15 @@
     again = [again_gather(number) for number in range(CHUNKS)]
     left[col] = x0_ref[...]
     right[row] = x0_ref[...]
-    chunks[0].begin()
-    across_rows.begin()
+    for gather in (across_rows, *chunks):
+        gather.begin()
     for i in range(rows // EDGE):
         for j in range(0, cols // EDGE, 2):
             mask[i * EDGE : (i + 1) * EDGE, j * EDGE : (j + 2) * EDGE] = block_masks(mask_ref, i, j)
     acc[...] = jnp.zeros_like(acc)
-    going, waiting = [across_rows, chunks[0]], chunks[1:]
+    going = [across_rows, *chunks]
     while going:
-        if waiting:
-            waiting[0].begin()
-        begun = waiting[:1]
-        waiting = waiting[1:]
+        begun = []
         for gather in list(going):
             if next(gather.going, "end") is None:
                 continue

time: 130 us -> 126 us (0.969)
  Pallas kernels: 129 us -> 125 us
    pallas_call x1, Pallas kernels: 76 us -> 72.1 us  [send_blocks_back(): pl.pallas_call(functools.partial(back_kernel, scale, outer, inner, row_co...]
where the time goes in v6:
time: 126 us
  Pallas kernels  125 us (99%)
    pallas_call x1, Pallas kernels, send_blocks_back(): pl.pallas_call(functools.partial(back_kernel, scale, outer, inner, row_co...  72.1 us
    pallas_call x1, Pallas kernels, send_blocks_out(): pl.pallas_call(functools.partial(send_kernel, outer, inner, row_count), o...  33.9 us
    pallas_call x1, Pallas kernels, grid_step(): pl.pallas_call(functools.partial(grid_kernel, chunk), out_shape=jax.Shape...  16.9 us

profile of v6, /device:TPU:1, one launch (start us, length us, event | category | flops | bytes accessed | tf_op | source)
XLA Modules:
  0.0 125.9 jit_solution(13446926645174368455)
XLA Ops:
  0.6 33.9 %send_out.1 = (bf16[32,8,32,128]{3,2,1,0:T(8,128)(2,1)}, s32[8,128]{1,0:T(8,128)}) custom-call(s32[8,32]{1,0:T(8,128)} %bitcast.9, s32[8,32]{1,0:T(8,128)} %bitcast.10, bf16[512,256]{1,0:T(8,128)(2,1)} %density_ref.1), custom_call_target="tpu_custom_call" | custom-call | tf_op jit(solution)/shard_map/send_out/pallas_call | solution.py:193
  34.5 16.9 %grid.1.slots_ref = bf16[32,8,32,128]{3,2,1,0:T(8,128)(2,1)} custom-call(s32[2,8,32]{2,1,0:T(8,128)} %bitcast.11, bf16[32,8,32,128]{3,2,1,0:T(8,128)(2,1)} %get-tuple-element.8.recv_ref, bf16[1024,2048]{1,0:T(8,128)(2,1)} %bitcast.8, f32[1,2048]{1,0:T(1,128)} %vloc_ref.1), custom_call_target="tpu_custom_call" | custom-call | tf_op jit(solution)/shard_map/grid/pallas_call | solution.py:488
  51.4 72.1 %back_and_sign.1 = (f32[512,256]{1,0:T(8,128)}, bf16[512,256]{1,0:T(8,128)(2,1)}, f32[512,256]{1,0:T(8,128)}) custom-call(s32[8,128]{1,0:T(8,128)} %get-tuple-element.7.kept_ref, s32[4,8]{1,0:T(4,128)} %bitcast.12, bf16[32,8,32,128]{3,2,1,0:T(8,128)(2,1)} %grid.1.slots_ref, f32[512,256]{1,0:T(8,128)} %core_ref.3), custom_call_target="tpu_custom_call" | custom-call | tf_op jit(solution)/shard_map/back_and_sign/pallas_call | solution.py:366
  123.6 2.3 %finish.1 = (f32[512,256]{1,0:T(8,128)}, f32[512,256]{1,0:T(8,128)}) custom-call(f32[512,256]{1,0:T(8,128)} %core_ref.3, f32[512,256]{1,0:T(8,128)} %get-tuple-element.9.ham_ref, bf16[512,256]{1,0:T(8,128)(2,1)} %get-tuple-element.10.x0_ref, f32[512,256]{1,0:T(8,128)} %get-tuple-element.11.x3_ref), custom_call_target="tpu_custom_call" | custom-call | tf_op jit(solution)/shard_map/finish/pallas_call | solution.py:729
